TPU v7x, 512 devices: a whole 4x4x16 slice. The times are simulated.
512 devices in a mesh: ctx: 32 (over z, core), head: 16 (over x, y).
Axes of the slice: x: 4, y: 4, z: 16, core: 2. Of those that a mesh axis runs over, the one named last changes fastest.
Arguments:
- queries: bfloat16 [12288, 2048], P(('ctx', 'head')), may hold values from -6 to 6
- keys: bfloat16 [12288, 2048], P(('ctx', 'head')), may hold values from -6 to 6
- values: bfloat16 [12288, 2048], P(('ctx', 'head')), may hold values from -6 to 6
- outputs: bfloat16 [12288, 2048], P(('ctx', 'head')), may hold values from -6 to 6
- grad_out: bfloat16 [12288, 2048], P(('ctx', 'head')), may hold values from -6 to 6
- log_sums: float32 [16, 12288], P('head', 'ctx')
- doc_ids: int32 [12288], P('ctx'), may hold values from 0 to 3, as said below
Outputs:
- grad_queries: bfloat16 [12288, 2048], P(('ctx', 'head'))
- grad_keys: bfloat16 [12288, 2048], P(('ctx', 'head'))
- grad_values: bfloat16 [12288, 2048], P(('ctx', 'head'))
Inputs may be any that keep to these rules, and one draw needn't show every extreme that they name: `doc_ids`: document numbers never fall along the tokens; there are 4 documents, each of 1 to 6144 tokens, one of exactly 6144 tokens; document 0 starts at token 0.
All inputs are finite; a program needn't handle non-finite values.
Results may differ from a plain program's by a relative error of at most 0.017.
Values may be sent and summed in bfloat16 or wider, within the bound.
A program may use at most 128 MiB of HBM per device.

v0:
```python
import jax
import jax.numpy as jnp
from jax import lax
from jax.sharding import PartitionSpec as P


def tile_terms(query_tile, key_tile, value_tile, grad_tile, lse_rows, delta_rows, allowed):
    softmax_scale = key_tile.shape[1] ** (-0.5)
    scores = jnp.dot(query_tile, key_tile.T, preferred_element_type=jnp.float32) * softmax_scale
    probs = jnp.exp(jnp.where(allowed, scores - lse_rows[:, None], -1e30))
    dprobs = jnp.dot(grad_tile, value_tile.T, preferred_element_type=jnp.float32)
    dscores = (probs * (dprobs - delta_rows[:, None])).astype(jnp.bfloat16)
    return (probs.astype(jnp.bfloat16), dscores)


def contract_rows(left, right):
    return lax.dot_general(
        left, right, (((0,), (0,)), ((), ())), preferred_element_type=jnp.float32
    )


def per_device(queries, keys, values, outputs, grad_out, log_sums, doc_ids):
    query_rows, key_rows, value_rows, out_rows, grad_rows = (
        lax.all_to_all(queries, "head", split_axis=1, concat_axis=0, tiled=True),
        lax.all_to_all(keys, "head", split_axis=1, concat_axis=0, tiled=True),
        lax.all_to_all(values, "head", split_axis=1, concat_axis=0, tiled=True),
        lax.all_to_all(outputs, "head", split_axis=1, concat_axis=0, tiled=True),
        lax.all_to_all(grad_out, "head", split_axis=1, concat_axis=0, tiled=True),
    )
    delta = jnp.sum(grad_rows.astype(jnp.float32) * out_rows.astype(jnp.float32), axis=1)
    local_rows = query_rows.shape[0]
    softmax_scale = query_rows.shape[1] ** (-0.5)
    row_first = lax.axis_index("ctx") * local_rows
    my_positions = row_first + jnp.arange(local_rows, dtype=jnp.int32)
    lse_mine = log_sums[0]
    all_docs = lax.all_gather(doc_ids, "ctx", axis=0, tiled=True)
    all_lse, all_delta = (
        lax.all_gather(lse_mine, "ctx", axis=0, tiled=True),
        lax.all_gather(delta, "ctx", axis=0, tiled=True),
    )
    empty = jnp.zeros(query_rows.shape, jnp.float32)
    pieces = (
        lax.all_gather(key_rows, "ctx", axis=0, tiled=True),
        lax.all_gather(value_rows, "ctx", axis=0, tiled=True),
    )
    key_piece = pieces[0]
    value_piece = pieces[1]
    piece_rows = key_piece.shape[0]

    def query_compute(total):
        col_pos = jnp.arange(piece_rows, dtype=jnp.int32)
        allowed = (col_pos[None, :] <= my_positions[:, None]) & (
            (all_docs[None, :] == doc_ids[:, None]) | (all_docs[None, :] == 0)
        )
        probs, dscores = tile_terms(
            query_rows, key_piece, value_piece, grad_rows, lse_mine, delta, allowed
        )
        return jnp.dot(dscores, key_piece, preferred_element_type=jnp.float32)

    def query_keep(total):
        return total

    grad_q = lax.cond(jnp.int32(0) < row_first + local_rows, query_compute, query_keep, empty)
    pieces = (
        lax.all_gather(query_rows, "ctx", axis=0, tiled=True),
        lax.all_gather(grad_rows, "ctx", axis=0, tiled=True),
    )
    query_piece = pieces[0]
    grad_piece = pieces[1]
    key_piece_rows = query_piece.shape[0]

    def key_compute(sums):
        row_pos = jnp.arange(key_piece_rows, dtype=jnp.int32)
        allowed = (my_positions[None, :] <= row_pos[:, None]) & (
            (doc_ids[None, :] == all_docs[:, None]) | (doc_ids[None, :] == 0)
        )
        probs, dscores = tile_terms(
            query_piece, key_rows, value_rows, grad_piece, all_lse, all_delta, allowed
        )
        return (contract_rows(dscores, query_piece), contract_rows(probs, grad_piece))

    def key_keep(sums):
        return sums

    grad_k, grad_v = lax.cond(
        jnp.int32(0) + key_piece_rows > row_first, key_compute, key_keep, (empty, empty)
    )
    grad_q = (grad_q * softmax_scale).astype(jnp.bfloat16)
    grad_k = (grad_k * softmax_scale).astype(jnp.bfloat16)
    grad_v = grad_v.astype(jnp.bfloat16)
    return (
        lax.all_to_all(grad_q, "head", split_axis=0, concat_axis=1, tiled=True),
        lax.all_to_all(grad_k, "head", split_axis=0, concat_axis=1, tiled=True),
        lax.all_to_all(grad_v, "head", split_axis=0, concat_axis=1, tiled=True),
    )


def solution(mesh):
    placed = (
        P(("ctx", "head"), None),
        P(("ctx", "head"), None),
        P(("ctx", "head"), None),
        P(("ctx", "head"), None),
        P(("ctx", "head"), None),
        P("head", "ctx"),
        P("ctx"),
    )
    return jax.shard_map(
        per_device,
        mesh=mesh,
        in_specs=placed,
        out_specs=(P(("ctx", "head"), None), P(("ctx", "head"), None), P(("ctx", "head"), None)),
        check_vma=False,
    )
```

profile of v0, /device:TPU:1, one launch (start us, length us, event | category | flops | bytes accessed | tf_op | source)
XLA Modules:
  0.0 388.6 jit_solution(11223790670937530275)
XLA Ops:
  7.2 0.0 all-gather.8.cloned.1.call-start
  7.2 0.8 copy-done
  8.1 14.1 %all_to_all.146 = bf16[24,16,128]{2,0,1:T(8,128)(2,1)} all-to-all(bf16[24,16,128]{2,0,1:T(8,128)(2,1)S(1)} %copy_bitcast_fusion.6), channel_id=1, replica_groups=mesh['ctx'=32,'head'=16] {'head'}, dimensions={1} | all-to-all | bytes 196608 | tf_op jit(solution)/shard_map/all_to_all | solution.py:25
  22.2 0.0 all-gather.8.cloned.1.call-update
  22.2 0.0 all-gather.10.cloned.1.call-start
  22.2 0.9 copy_bitcast_fusion.4
  23.2 9.8 %all_to_all.147 = bf16[24,16,128]{2,0,1:T(8,128)(2,1)} all-to-all(bf16[24,16,128]{2,0,1:T(8,128)(2,1)S(1)} %copy_bitcast_fusion.4), channel_id=1, replica_groups=mesh['ctx'=32,'head'=16] {'head'}, dimensions={1} | all-to-all | bytes 196608 | tf_op jit(solution)/shard_map/all_to_all | solution.py:26
  33.0 0.0 all-gather.10.cloned.1.call-update
  33.0 0.0 all-gather.12.cloned.1.call-start
  33.1 0.9 copy_bitcast_fusion.7
  34.0 9.9 %all_to_all.148 = bf16[24,16,128]{2,0,1:T(8,128)(2,1)} all-to-all(bf16[24,16,128]{2,0,1:T(8,128)(2,1)S(1)} %copy_bitcast_fusion.7), channel_id=1, replica_groups=mesh['ctx'=32,'head'=16] {'head'}, dimensions={1} | all-to-all | bytes 196608 | tf_op jit(solution)/shard_map/all_to_all | solution.py:24
  43.9 0.0 all-gather.12.cloned.1.call-update
  43.9 0.0 all-gather.14.cloned.1.call-start
  43.9 0.9 copy_bitcast_fusion.5
  44.8 9.8 %all_to_all.149 = bf16[24,16,128]{2,0,1:T(8,128)(2,1)} all-to-all(bf16[24,16,128]{2,0,1:T(8,128)(2,1)S(1)} %copy_bitcast_fusion.5), channel_id=1, replica_groups=mesh['ctx'=32,'head'=16] {'head'}, dimensions={1} | all-to-all | bytes 196608 | tf_op jit(solution)/shard_map/all_to_all | solution.py:28
  54.7 0.0 all-gather.14.cloned.1.call-update
  54.7 1.6 copy_bitcast_fusion.3
  56.3 3.5 all-to-all-start.4
  59.8 0.7 reshape.46
  60.5 42.2 %all-gather.1 = s32[32,1,384]{2,1,0:T(1,128)S(1)} all-gather(s32[1,1,384]{2,1,0:T(1,128)S(1)} %reshape.46), channel_id=1, replica_groups=mesh['ctx'=32,'head'=16] {'ctx'}, dimensions={0}, use_global_device_ids=true | all-gather | bytes 50688 | tf_op jit(solution)/shard_map/all_gather | solution.py:36
  102.7 29.0 %all-gather = f32[1,12288]{1,0:T(1,128)} all-gather(f32[1,384]{1,0:T(1,128)} %param.16), channel_id=2, replica_groups=mesh['ctx'=32,'head'=16] {'ctx'}, dimensions={1}, use_global_device_ids=true | all-gather | bytes 50688 | tf_op jit(solution)/shard_map/all_gather | solution.py:38
  131.7 1.0 fusion.8
  132.8 0.1 reshape.48
  132.9 30.6 %all-gather.2 = f32[32,1,384]{2,1,0:T(1,128)} all-gather(f32[1,1,384]{2,1,0:T(1,128)S(1)} %reshape.48), channel_id=1, replica_groups=mesh['ctx'=32,'head'=16] {'ctx'}, dimensions={0}, use_global_device_ids=true | all-gather | bytes 50688 | tf_op jit(solution)/shard_map/all_gather | solution.py:39
  163.5 6.6 %all-gather.10.cloned.1.call-done = bf16[12288,128]{1,0:T(8,128)(2,1)} async-done(((bf16[384,128]{1,0:T(8,128)(2,1)}), bf16[12288,128]{1,0:T(8,128)(2,1)}) %all-gather.10.cloned.1.call-update) | async-done | bytes 3145744 | tf_op jit(solution)/shard_map/all_gather | solution.py:44
  170.1 29.5 %conditional.2 = (f32[384,128]{1,0:T(8,128)}) conditional(s32[]{:T(128)} %convert_element_type.35, () %tuple.22, (s32[384]{0:T(512)S(1)}, s32[12288]{0:T(1024)S(1)}, s32[384]{0:T(512)}, bf16[384,128]{1,0:T(8,128)(2,1)}, bf16[12288,128]{1,0:T(8,128)(2,1)}, /*index=5*/f32[1,384]{1,0:T(1,128)}, bf16[384,128]{1,0:T(8,128)(2,1)}, ...), branch_computations={%region_1.0_spmd, %region_2.3_spmd} | conditional | flops 3671076864 | bytes 60702844 | solution.py:63
  170.1 11.2 %fusion.9 = f32[384,12288]{1,0:T(8,128)} fusion(bf16[384,128]{1,0:T(8,128)(2,1)} %get-tuple-element.42, bf16[12288,128]{1,0:T(8,128)(2,1)} %get-tuple-element.43), kind=kOutput, calls=%fused_computation.28 | convolution fusion | flops 1207959552 | bytes 22118400 | tf_op jit(solution)/shard_map/cond/branch_1_fun/dot_general | solution.py:9
  181.3 0.1 reduce_sum.13
  181.4 18.2 %fusion.5 = f32[384,128]{1,0:T(8,128)} fusion(bf16[12288,128]{1,0:T(8,128)(2,1)S(1)} %copy-done.2, f32[384,12288]{1,0:T(8,128)} %fusion.9, bf16[384,128]{1,0:T(8,128)(2,1)S(1)} %copy-done.4, bf16[12288,128]{1,0:T(8,128)(2,1)} %get-tuple-element.46, f32[384]{0:T(512)S(1)} %reduce_sum.13, f32[384]{0:T(512)S(1)} %reduce.1, s32[12288]{0:T(1024)S(1)} %get-tuple-element.40, ...), kind=kOutput, calls=%fused_computation.11 | convolution fusion | flops 2463105024 | bytes 25528320 | tf_op jit(solution)/shard_map/cond/branch_1_fun/dot_general | solution.py:58
  199.6 1.6 multiply_convert_fusion.3
  201.2 6.7 %all-to-all-start.5 = ((bf16[16,24,128]{2,1,0:T(8,128)(2,1)}), bf16[16,24,128]{2,1,0:T(8,128)(2,1)}, u32[]{:S(2)}, u32[]{:S(2)}) async-start(bf16[16,24,128]{2,1,0:T(8,128)(2,1)} %bitcast.10), calls=%async_computation.5 | async-start | bytes 196608 | tf_op jit(solution)/shard_map/all_to_all | solution.py:92
  207.9 34.6 %all-gather.12.cloned.1.call-done = bf16[12288,128]{1,0:T(8,128)(2,1)} async-done(((bf16[384,128]{1,0:T(8,128)(2,1)}), bf16[12288,128]{1,0:T(8,128)(2,1)}) %all-gather.12.cloned.1.call-update) | async-done | bytes 3145744 | tf_op jit(solution)/shard_map/all_gather | solution.py:65
  242.5 72.0 %all-gather.14.cloned.1.call-done = bf16[12288,128]{1,0:T(8,128)(2,1)} async-done(((bf16[384,128]{1,0:T(8,128)(2,1)}), bf16[12288,128]{1,0:T(8,128)(2,1)}) %all-gather.14.cloned.1.call-update) | async-done | bytes 3145744 | tf_op jit(solution)/shard_map/all_gather | solution.py:66
  314.5 41.4 %conditional.3 = (f32[384,128]{1,0:T(8,128)S(1)}, f32[384,128]{1,0:T(8,128)}) conditional(s32[]{:T(128)} %convert_element_type.40, () %tuple.24, (s32[384]{0:T(512)S(1)}, s32[384]{0:T(512)}, s32[12288]{0:T(1024)S(1)}, bf16[12288,128]{1,0:T(8,128)(2,1)}, bf16[384,128]{1,0:T(8,128)(2,1)}, /*index=5*/f32[12288]{0:T(1024)}, bf16[12288,128]{1,0:T(8,128)(2,1)}, ...), branch_computations={%region_3.4_spmd, %region_4.5_spmd} | conditional | flops 4883743232 | bytes 82728264 | solution.py:85
  314.5 0.6 copy-done.5
  315.1 0.7 broadcast_compare_fusion
  315.8 13.4 %select_exponential_fusion = f32[12288,384]{1,0:T(8,128)} fusion(bf16[12288,128]{1,0:T(8,128)(2,1)} %get-tuple-element.51, bf16[384,128]{1,0:T(8,128)(2,1)} %get-tuple-element.52, f32[12288]{0:T(1024)} %get-tuple-element.53, s32[384]{0:T(512)} %get-tuple-element.49, s32[384]{0:T(512)S(1)} %get-tuple-element.48, s32[12288]{0:T(1024)} %copy-done.5, ...), kind=kOutput, calls=%fused_computation.1 | convolution fusion | flops 1240989696 | bytes 22220160 | tf_op jit(solution)/shard_map/cond/branch_1_fun/dot_general | solution.py:9
  329.2 16.9 %fusion.3 = f32[384,128]{1,0:T(8,128)S(1)} fusion(bf16[12288,128]{1,0:T(8,128)(2,1)} %get-tuple-element.51, f32[12288,384]{1,0:T(8,128)} %select_exponential_fusion, bf16[12288,128]{1,0:T(8,128)(2,1)S(1)} %copy-done.1, bf16[384,128]{1,0:T(8,128)(2,1)S(1)} %get-tuple-element.55, f32[12288]{0:T(1024)} %get-tuple-element.56), kind=kOutput, calls=%fused_computation.6 | convolution fusion | flops 2430074880 | bytes 25509888 | tf_op jit(solution)/shard_map/cond/branch_1_fun/dot_general | solution.py:17
  346.2 9.7 %fusion.1 = f32[384,128]{1,0:T(8,128)} fusion(bf16[12288,128]{1,0:T(8,128)(2,1)S(1)} %copy-done.1, f32[12288,384]{1,0:T(8,128)} %select_exponential_fusion), kind=kOutput, calls=%fused_computation.4 | convolution fusion | flops 1212678144 | bytes 22216704 | tf_op jit(solution)/shard_map/cond/branch_1_fun/dot_general | solution.py:17
  355.9 0.7 multiply_convert_fusion.2
  356.5 1.6 convert_element_type.42
  358.1 6.5 %all-to-all-start.6 = ((bf16[16,24,128]{2,1,0:T(8,128)(2,1)}), bf16[16,24,128]{2,1,0:T(8,128)(2,1)S(1)}, u32[]{:S(2)}, u32[]{:S(2)}) async-start(bf16[16,24,128]{2,1,0:T(8,128)(2,1)} %bitcast.18), calls=%async_computation.6 | async-start | bytes 196608 | tf_op jit(solution)/shard_map/all_to_all | solution.py:93
  364.6 1.5 copy_bitcast_fusion.2
  366.2 5.1 %all-to-all-done.6 = bf16[16,24,128]{2,1,0:T(8,128)(2,1)S(1)} async-done(((bf16[16,24,128]{2,1,0:T(8,128)(2,1)}), bf16[16,24,128]{2,1,0:T(8,128)(2,1)S(1)}, u32[]{:S(2)}, u32[]{:S(2)}) %all-to-all-start.6) | async-done | bytes 98336 | tf_op jit(solution)/shard_map/all_to_all | solution.py:93
  371.2 3.5 all-to-all-start.7
  374.8 0.6 copy_bitcast_fusion.1
  375.4 5.9 %all-to-all-done.7 = bf16[16,24,128]{2,1,0:T(8,128)(2,1)S(1)} async-done(((bf16[16,24,128]{2,1,0:T(8,128)(2,1)}), bf16[16,24,128]{2,1,0:T(8,128)(2,1)S(1)}, u32[]{:S(2)}, u32[]{:S(2)}) %all-to-all-start.7) | async-done | bytes 98336 | tf_op jit(solution)/shard_map/all_to_all | solution.py:94
  381.4 0.6 copy_bitcast_fusion
  (21 shorter events, 0.1 us)
Async XLA Ops:
  7.2 0.9 copy-start
  7.2 156.3 %all-gather.8.cloned.1.call-start = ((), (), s32[]{:S(2)}) async-start(), calls=%async_computation.8 | async-start | bytes 3244032 | tf_op jit(solution)/shard_map/all_gather | solution.py:43
  22.2 147.9 %all-gather.10.cloned.1.call-start = ((), (), s32[]{:S(2)}) async-start(), calls=%async_computation.9 | async-start | bytes 3244032 | tf_op jit(solution)/shard_map/all_gather | solution.py:44
  33.0 209.4 %all-gather.12.cloned.1.call-start = ((), (), s32[]{:S(2)}) async-start(), calls=%async_computation.10 | async-start | bytes 3244032 | tf_op jit(solution)/shard_map/all_gather | solution.py:65
  43.9 270.6 %all-gather.14.cloned.1.call-start = ((), (), s32[]{:S(2)}) async-start(), calls=%async_computation.11 | async-start | bytes 3244032 | tf_op jit(solution)/shard_map/all_gather | solution.py:66
  56.3 75.5 %all-to-all-start.4 = ((bf16[24,16,128]{2,0,1:T(8,128)(2,1)}), bf16[24,16,128]{2,0,1:T(8,128)(2,1)S(1)}, u32[]{:S(2)}, u32[]{:S(2)}) async-start(bf16[24,16,128]{2,0,1:T(8,128)(2,1)} %copy_bitcast_fusion.3), calls=%async_computation.4 | async-start | bytes 196608 | tf_op jit(solution)/shard_map/all_to_all | solution.py:27
  170.1 144.4 %copy-start.3 = (bf16[24,16,128]{2,0,1:T(8,128)(2,1)S(1)}, bf16[24,16,128]{2,0,1:T(8,128)(2,1)}, u32[]{:S(2)}) copy-start(bf16[24,16,128]{2,0,1:T(8,128)(2,1)} %all_to_all.147) | copy-start | bytes 294916
  170.1 11.3 %copy-start.7 = (f32[1,384]{1,0:T(1,128)S(1)}, f32[1,384]{1,0:T(1,128)}, u32[]{:S(2)}) copy-start(f32[1,384]{1,0:T(1,128)} %get-tuple-element.44) | copy-start | bytes 4612 | tf_op jit(solution)/shard_map/cond
  170.1 11.3 %copy-start.2 = (bf16[12288,128]{1,0:T(8,128)(2,1)S(1)}, bf16[12288,128]{1,0:T(8,128)(2,1)}, u32[]{:S(2)}) copy-start(bf16[12288,128]{1,0:T(8,128)(2,1)} %get-tuple-element.43) | copy-start | bytes 9437188 | tf_op jit(solution)/shard_map/cond
  170.1 11.3 %copy-start.4 = (bf16[384,128]{1,0:T(8,128)(2,1)S(1)}, bf16[384,128]{1,0:T(8,128)(2,1)}, u32[]{:S(2)}) copy-start(bf16[384,128]{1,0:T(8,128)(2,1)} %get-tuple-element.45) | copy-start | bytes 294916 | tf_op jit(solution)/shard_map/cond
  170.1 11.3 %copy-start.6 = (s32[384]{0:T(512)S(1)}, s32[384]{0:T(512)}, u32[]{:S(2)}) copy-start(s32[384]{0:T(512)} %get-tuple-element.41) | copy-start | bytes 4612 | tf_op jit(solution)/shard_map/cond
  201.2 156.9 %all-to-all-start.5 = ((bf16[16,24,128]{2,1,0:T(8,128)(2,1)}), bf16[16,24,128]{2,1,0:T(8,128)(2,1)}, u32[]{:S(2)}, u32[]{:S(2)}) async-start(bf16[16,24,128]{2,1,0:T(8,128)(2,1)} %bitcast.10), calls=%async_computation.5 | async-start | bytes 196608 | tf_op jit(solution)/shard_map/all_to_all | solution.py:92
  314.5 0.6 copy-start.5
  315.8 13.4 %copy-start.1 = (bf16[12288,128]{1,0:T(8,128)(2,1)S(1)}, bf16[12288,128]{1,0:T(8,128)(2,1)}, u32[]{:S(2)}) copy-start(bf16[12288,128]{1,0:T(8,128)(2,1)} %get-tuple-element.54) | copy-start | bytes 9437188 | tf_op jit(solution)/shard_map/cond
  358.1 13.1 %all-to-all-start.6 = ((bf16[16,24,128]{2,1,0:T(8,128)(2,1)}), bf16[16,24,128]{2,1,0:T(8,128)(2,1)S(1)}, u32[]{:S(2)}, u32[]{:S(2)}) async-start(bf16[16,24,128]{2,1,0:T(8,128)(2,1)} %bitcast.18), calls=%async_computation.6 | async-start | bytes 196608 | tf_op jit(solution)/shard_map/all_to_all | solution.py:93
  371.2 10.1 %all-to-all-start.7 = ((bf16[16,24,128]{2,1,0:T(8,128)(2,1)}), bf16[16,24,128]{2,1,0:T(8,128)(2,1)S(1)}, u32[]{:S(2)}, u32[]{:S(2)}) async-start(bf16[16,24,128]{2,1,0:T(8,128)(2,1)} %bitcast.20), calls=%async_computation.7 | async-start | bytes 196608 | tf_op jit(solution)/shard_map/all_to_all | solution.py:94
Sparse Core Ops, SparseCore 0:
  22.3 75.8 all-gather.7
  100.3 69.7 all-gather.9
  172.2 70.2 all-gather.11
  244.5 69.9 all-gather.13
where the time goes:
time: 390 us; the launch traced here: 389 us
  blocking collectives  145 us (37%)
  waiting for transfers between devices  124 us (32%)
  matrix products  69.4 us (18%)
  starting transfers between devices  20.4 us (5%)
  between operations  13.8 us (4%)
  local copies, waits for them, and re-layouts  9.49 us (2%)
  other arithmetic  5.54 us (1%)
    all_gather x1, waiting for transfers between devices, per_device(): lax.all_gather(grad_rows, 'ctx', axis=0, tiled=True)  72 us
    all_gather x1, blocking collectives, per_device(): all_docs = lax.all_gather(doc_ids, 'ctx', axis=0, tiled=True)  42.2 us
    all_gather x1, waiting for transfers between devices, per_device(): lax.all_gather(query_rows, 'ctx', axis=0, tiled=True)  34.6 us
    all_gather x1, blocking collectives, per_device(): lax.all_gather(delta, 'ctx', axis=0, tiled=True)  30.6 us
    all_gather x1, blocking collectives, per_device(): lax.all_gather(lse_mine, 'ctx', axis=0, tiled=True)  29 us
    dot_general x2, matrix products, contract_rows(): lax.dot_general(left, right, (((0,), (0,)), ((), ())), preferred_element_...  26.6 us
    dot_general x2, matrix products, tile_terms(): jnp.dot(query_tile, key_tile.T, preferred_element_type=jnp.float32)  24.6 us
    dot_general x1, matrix products, query_compute(): return jnp.dot(dscores, key_piece, preferred_element_type=jnp.float32)  18.2 us
  transfers between devices with their start and end apart: 8, of which 5 were waited for; matrix products, arithmetic and copies ran while one was open for 21% of the time, Pallas kernels for 0%

commit v1 on v0

v1 whole, which is shorter than its diff:
```python
import jax
import jax.numpy as jnp
from jax import lax
from jax.experimental import pallas as pl
from jax.experimental.pallas import tpu as pltpu
from jax.sharding import PartitionSpec as P

DH = 128
NX, NY, NZ, NC = 4, 4, 16, 2
ROWS = 24
CTX_ROWS = NX * NY * ROWS
SPAN = NC * CTX_ROWS
Q_Z = NC * NY * ROWS
K_Z = NX * ROWS
Q_BLK = 2 * Q_Z
K_BLK = 2 * K_Z
N_BLK = NZ // 2
MESH = pl.DeviceIdType.MESH
F32 = jnp.float32
BF16 = jnp.bfloat16


def here():
    ctx, head = lax.axis_index("ctx"), lax.axis_index("head")
    return lax.div(head, NY), lax.rem(head, NY), lax.div(ctx, NC), lax.rem(ctx, NC)


def device(x, y, z, c):
    return (z * NC + c, x * NY + y)


def ring(me, step, size):
    away = lax.div(step, 2) + 1
    return lax.rem(jnp.where(lax.rem(step, 2) == 0, me + away, me - away + size), size)


def columns(head):
    return pl.ds(pl.multiple_of(head * DH, DH), DH)


def remote(src, dst, send, recv, to):
    return pltpu.make_async_remote_copy(
        src_ref=src, dst_ref=dst, send_sem=send, recv_sem=recv, device_id=to, device_id_type=MESH
    )


def loop(count, body):
    def step(i, carry):
        body(i)
        return carry

    lax.fori_loop(0, count, step, 0)


def gather_kernel(
    q, k, v, o, g, lse, doc,
    Q, K, V, G, L, D, C,
    delta,
    z_send, z_recv, own, d_send, d_recv, c_send, c_recv,
    hub_send, hub_recv, plane_send, plane_recv,
    x_send, x_recv, y_send, y_recv, s_send, s_recv,
):
    x, y, z, c = here()
    plane = x * NY + y
    sib = device(x, y, z, 1 - c)
    hub = z == plane
    zplane = lax.rem(z, NX * NY)
    hx, hy = lax.div(zplane, NY), lax.rem(zplane, NY)

    barrier = pltpu.get_barrier_semaphore()

    def greet(to):
        pl.semaphore_signal(barrier, inc=1, device_id=to, device_id_type=MESH)

    loop(NZ - 1, lambda i: greet(device(x, y, ring(z, i, NZ), c)))
    loop(NX - 1, lambda i: greet(device(ring(x, i, NX), y, z, c)))
    loop(NY - 1, lambda i: greet(device(x, ring(y, i, NY), z, c)))
    greet(sib)

    def plane_peer(i):
        other = lax.rem(plane + i + 1, NX * NY)
        return device(lax.div(other, NY), lax.rem(other, NY), z, c)

    @pl.when(hub)
    def _():
        loop(NX * NY - 1, lambda i: greet(plane_peer(i)))

    @pl.when(jnp.logical_not(hub))
    def _():
        greet(device(hx, hy, z, c))

    base = NZ - 1 + NX - 1 + NY - 1 + 1
    pl.semaphore_wait(barrier, base + jnp.where(hub, NX * NY - 1, 1))

    srcs = (k, v, q, g)

    def landing(a, zs):
        return (K.at[zs, x], V.at[zs, x], Q.at[zs, c, y], G.at[zs, c, y])[a]

    def z_copy(a, i):
        to = ring(z, i, NZ)
        return remote(
            srcs[a].at[:, columns(to)], landing(a, z), z_send.at[a, i], z_recv.at[a, z],
            device(x, y, to, c),
        )

    def own_copy(a):
        return pltpu.make_async_copy(srcs[a].at[:, columns(z)], landing(a, z), own.at[a])

    for a in range(4):
        own_copy(a).start()
        loop(NZ - 1, lambda i, a=a: z_copy(a, i).start())

    lse_own = pltpu.make_async_copy(lse, L.at[c, z], own.at[4])

    def lse_copy(to, frm):
        return remote(lse, L.at[c, z], hub_send, hub_recv.at[frm], device(x, y, to, c))

    @pl.when(hub)
    def _():
        lse_own.start()

    @pl.when(jnp.logical_not(hub))
    def _():
        lse_copy(plane, z).start()

    doc_own = pltpu.make_async_copy(doc, C.at[c, z], own.at[5])
    doc_own.start()

    def doc_copy(i, frm):
        return remote(doc, C.at[c, z], c_send.at[i], c_recv.at[frm], device(x, y, ring(z, i, NZ), c))

    loop(NZ - 1, lambda i: doc_copy(i, z).start())

    lane = lax.broadcasted_iota(jnp.int32, (ROWS, DH), 1)
    sums = jnp.zeros((ROWS, DH), F32)
    for h in range(NZ):
        cols = slice(h * DH, (h + 1) * DH)
        row = jnp.sum(g[:, cols].astype(F32) * o[:, cols].astype(F32), axis=1, keepdims=True)
        sums = jnp.where(lane == h, row, sums)
    turned = jnp.concatenate([sums, jnp.zeros((DH - ROWS, DH), F32)], axis=0).T
    for h in range(NZ):
        delta[h] = turned[h : h + 1, :]

    def delta_copy(i):
        to = ring(z, i, NZ)
        return remote(delta.at[to], D.at[z, c, y], d_send.at[i], d_recv.at[z], device(x, y, to, c))

    delta_own = pltpu.make_async_copy(delta.at[z], D.at[z, c, y], own.at[6])
    delta_own.start()
    loop(NZ - 1, lambda i: delta_copy(i).start())

    def z_wait(a):
        own_copy(a).wait()

        def one(i):
            frm = ring(z, i, NZ)
            remote(
                srcs[a].at[:, columns(frm)], landing(a, frm), z_send.at[a, i], z_recv.at[a, frm], sib
            ).wait_recv()

        loop(NZ - 1, one)

    def x_copy(a, i, frm, to):
        part = (K, V)[a].at[:, frm]
        return remote(part, part, x_send.at[a, i], x_recv.at[a, frm], device(to, y, z, c))

    for a in range(2):
        z_wait(a)
        for i in range(NX - 1):
            x_copy(a, i, x, ring(x, i, NX)).start()

    def plane_copy(i):
        return remote(L.at[c], L.at[c], plane_send.at[i], plane_recv, plane_peer(i))

    def sib_copy(part, slot):
        return remote(part, part, s_send.at[slot], s_recv.at[slot], sib)

    @pl.when(hub)
    def _():
        lse_own.wait()

        def one(i):
            frm = ring(z, i, NZ)
            remote(lse, L.at[c, frm], hub_send, hub_recv.at[frm], sib).wait_recv()

        loop(NZ - 1, one)
        loop(NX * NY - 1, lambda i: plane_copy(i).start())

    ys = (Q, G, D)

    def y_copy(a, i, frm, to):
        part = ys[a].at[:, c, frm]
        return remote(part, part, y_send.at[a, i], y_recv.at[a, frm], device(x, to, z, c))

    def sib_y(a, frm, core):
        return sib_copy(ys[a].at[:, core, frm], a * NY + frm)

    delta_own.wait()
    loop(
        NZ - 1,
        lambda i: remote(
            delta.at[z], D.at[ring(z, i, NZ), c, y], d_send.at[i], d_recv.at[ring(z, i, NZ)], sib
        ).wait_recv(),
    )
    for a in (2, 0, 1):
        if a < 2:
            z_wait(2 + a)
        for i in range(NY - 1):
            y_copy(a, i, y, ring(y, i, NY)).start()
        sib_y(a, y, c).start()

    doc_own.wait()
    loop(
        NZ - 1,
        lambda i: remote(doc, C.at[c, ring(z, i, NZ)], c_send.at[i], c_recv.at[ring(z, i, NZ)], sib).wait_recv(),
    )
    sib_copy(C.at[c], 3 * NY).start()

    @pl.when(jnp.logical_not(hub))
    def _():
        remote(L.at[c], L.at[c], plane_send.at[0], plane_recv, sib).wait_recv()

    sib_copy(L.at[c], 3 * NY + 1).start()

    for a in (2, 0, 1):
        for i in range(NY - 1):
            frm = ring(y, i, NY)
            y_copy(a, i, frm, y).wait_recv()
            sib_y(a, frm, c).start()

    for a in range(2):
        for i in range(NX - 1):
            x_copy(a, i, ring(x, i, NX), x).wait_recv()
    for a in range(3):
        for frm in range(NY):
            sib_y(a, frm, 1 - c).wait_recv()
    sib_copy(C.at[1 - c], 3 * NY).wait_recv()
    sib_copy(L.at[1 - c], 3 * NY + 1).wait_recv()

    for a in range(4):
        loop(NZ - 1, lambda i, a=a: z_copy(a, i).wait_send())
    loop(NZ - 1, lambda i: doc_copy(i, z).wait_send())
    loop(NZ - 1, lambda i: delta_copy(i).wait_send())

    @pl.when(jnp.logical_not(hub))
    def _():
        lse_copy(plane, z).wait_send()

    @pl.when(hub)
    def _():
        loop(NX * NY - 1, lambda i: plane_copy(i).wait_send())

    for a in range(2):
        for i in range(NX - 1):
            x_copy(a, i, x, ring(x, i, NX)).wait_send()
    for a in range(3):
        for i in range(NY - 1):
            y_copy(a, i, y, ring(y, i, NY)).wait_send()
        for frm in range(NY):
            sib_y(a, frm, c).wait_send()
    sib_copy(C.at[c], 3 * NY).wait_send()
    sib_copy(L.at[c], 3 * NY + 1).wait_send()


def gather_inputs(q, k, v, o, g, lse, doc):
    dma = pltpu.SemaphoreType.DMA
    vmem = pl.BlockSpec(memory_space=pltpu.VMEM)
    hbm = pl.BlockSpec(memory_space=pl.ANY)
    kv = jax.ShapeDtypeStruct((NZ, NX, ROWS, DH), BF16)
    qg = jax.ShapeDtypeStruct((NZ, NC, NY, ROWS, DH), BF16)
    return pl.pallas_call(
        gather_kernel,
        out_shape=(
            qg, kv, kv, qg,
            jax.ShapeDtypeStruct((NC, NZ, 1, CTX_ROWS), F32),
            jax.ShapeDtypeStruct((NZ, NC, NY, 1, DH), F32),
            jax.ShapeDtypeStruct((NC, NZ, 1, CTX_ROWS), jnp.int32),
        ),
        in_specs=[vmem] * 7,
        out_specs=(hbm,) * 7,
        scratch_shapes=[
            pltpu.VMEM((NZ, 1, DH), F32),
            dma((4, NZ - 1)), dma((4, NZ)), dma((7,)),
            dma((NZ - 1,)), dma((NZ,)), dma((NZ - 1,)), dma((NZ,)),
            dma, dma((NZ,)), dma((NX * NY - 1,)), dma,
            dma((2, NX - 1)), dma((2, NX)), dma((3, NY - 1)), dma((3, NY)),
            dma((3 * NY + 2,)), dma((3 * NY + 2,)),
        ],
        compiler_params=pltpu.CompilerParams(collective_id=0, has_side_effects=True),
        name="gather_inputs",
    )(q, k, v, o, g, lse, doc)


def contract_last(left, right):
    return lax.dot_general(left, right, (((1,), (1,)), ((), ())), preferred_element_type=F32)


def contract_first(left, right):
    return lax.dot_general(left, right, (((0,), (0,)), ((), ())), preferred_element_type=F32)


def tile_kernel(Q, K, V, G, L, D, C, dQ, dK, dV, ks, vs, lse_s, delta_s, acc_k, acc_v):
    x, y, z, c = here()
    docs = C[...]
    ends = [jnp.sum((docs < d).astype(jnp.int32)) for d in (1, 2, 3)]

    def doc_start(pos):
        start = jnp.where(pos >= ends[0], ends[0], 0)
        start = jnp.where(pos >= ends[1], ends[1], start)
        return jnp.where(pos >= ends[2], ends[2], start)

    acc_k[...] = jnp.zeros_like(acc_k)
    acc_v[...] = jnp.zeros_like(acc_v)

    def gather_keys(i, carry):
        at = pl.ds(pl.multiple_of(i * K_BLK, K_BLK), K_BLK)
        ks[at, :] = K[pl.ds(2 * i, 2)].astype(F32).reshape(K_BLK, DH).astype(BF16)
        vs[at, :] = V[pl.ds(2 * i, 2)].astype(F32).reshape(K_BLK, DH).astype(BF16)
        return carry

    lax.fori_loop(0, N_BLK, gather_keys, 0)

    part = NY * ROWS
    lses, deltas = [], []
    for core in range(NC):
        mine = jnp.concatenate([L[core, zz] for zz in range(NZ)], axis=0)
        picked = mine[:, :part]
        for xx in range(1, NX):
            picked = jnp.where(x == xx, mine[:, xx * part : (xx + 1) * part], picked)
        lses.append(picked)
        for yy in range(NY):
            rows = jnp.concatenate([D[zz, core, yy] for zz in range(NZ)], axis=0)
            deltas.append(rows[:, :ROWS])
    lses = jnp.concatenate(lses, axis=1)
    deltas = jnp.concatenate(deltas, axis=1)
    for j in range(N_BLK):
        lse_s[j] = jnp.concatenate([lses[2 * j : 2 * j + 1], lses[2 * j + 1 : 2 * j + 2]], axis=1)
        delta_s[j] = jnp.concatenate([deltas[2 * j : 2 * j + 1], deltas[2 * j + 1 : 2 * j + 2]], axis=1)

    q_at = lax.broadcasted_iota(jnp.int32, (1, Q_BLK), 1)
    q_in = lax.rem(q_at, Q_Z)
    q_base = (
        lax.div(q_at, Q_Z) * SPAN + lax.div(q_in, part) * CTX_ROWS + x * part + lax.rem(q_in, part)
    )
    k_at = lax.broadcasted_iota(jnp.int32, (K_BLK, 1), 0)
    k_in = lax.rem(k_at, K_Z)
    k_base = (
        lax.div(k_at, K_Z) * SPAN
        + c * CTX_ROWS
        + lax.div(k_in, ROWS) * part
        + y * ROWS
        + lax.rem(k_in, ROWS)
    )
    scale = DH**-0.5

    def query_block(j, carry):
        qb = Q[pl.ds(2 * j, 2)].astype(F32).reshape(Q_BLK, DH).astype(BF16)
        gb = G[pl.ds(2 * j, 2)].astype(F32).reshape(Q_BLK, DH).astype(BF16)
        q_pos = q_base + j * (2 * SPAN)
        start = doc_start(q_pos)
        lse, delta = lse_s[j], delta_s[j]

        def tile(i, causal):
            at = pl.ds(pl.multiple_of(i * K_BLK, K_BLK), K_BLK)
            kb, vb = ks[at, :], vs[at, :]
            k_pos = k_base + i * (2 * SPAN)
            key = jnp.where(k_pos < ends[0], NZ * SPAN, k_pos)
            allowed = key >= start
            if causal:
                allowed = allowed & (k_pos <= q_pos)
            s = contract_last(kb, qb) * scale - lse
            p = jnp.where(allowed, jnp.exp(s), 0.0)
            ds = (p * (contract_last(vb, gb) - delta)).astype(BF16)
            acc_v[at, :] += jnp.dot(p.astype(BF16), gb, preferred_element_type=F32)
            acc_k[at, :] += jnp.dot(ds, qb, preferred_element_type=F32)
            return contract_first(ds, kb)

        total = lax.fori_loop(
            0, j, lambda i, t: t + tile(i, False), jnp.zeros((Q_BLK, DH), F32)
        )
        total = total + tile(j, True)
        dQ[pl.ds(2 * j, 2)] = total.reshape(2, NC, NY, ROWS, DH).astype(BF16)
        return carry

    lax.fori_loop(0, N_BLK, query_block, 0)
    for zz in range(NZ):
        at = slice(zz * K_Z, (zz + 1) * K_Z)
        dK[zz] = acc_k[at, :].reshape(NX, ROWS, DH).astype(BF16)
        dV[zz] = acc_v[at, :].reshape(NX, ROWS, DH).astype(BF16)


def tile_grads(Q, K, V, G, L, D, C):
    vmem = pl.BlockSpec(memory_space=pltpu.VMEM)
    kv = jax.ShapeDtypeStruct((NZ, NX, ROWS, DH), BF16)
    qg = jax.ShapeDtypeStruct((NZ, NC, NY, ROWS, DH), BF16)
    return pl.pallas_call(
        tile_kernel,
        out_shape=(qg, kv, kv),
        in_specs=[vmem] * 7,
        out_specs=(vmem,) * 3,
        scratch_shapes=[
            pltpu.VMEM((NZ * K_Z, DH), BF16),
            pltpu.VMEM((NZ * K_Z, DH), BF16),
            pltpu.VMEM((N_BLK, 1, Q_BLK), F32),
            pltpu.VMEM((N_BLK, 1, Q_BLK), F32),
            pltpu.VMEM((NZ * K_Z, DH), F32),
            pltpu.VMEM((NZ * K_Z, DH), F32),
        ],
        compiler_params=pltpu.CompilerParams(vmem_limit_bytes=48 * 1024 * 1024),
        name="tile_grads",
    )(Q, K, V, G, L, D, C)


def return_kernel(
    dQ, dK, dV, oq, ok, ov, rq, rk, rv, res,
    q_send, q_recv, k_send, k_recv, own, z_send, z_recv,
):
    x, y, z, c = here()
    barrier = pltpu.get_barrier_semaphore()

    def greet(to):
        pl.semaphore_signal(barrier, inc=1, device_id=to, device_id_type=MESH)

    def q_peer(i):
        other = lax.rem(y * NC + c + i + 1, NY * NC)
        return lax.div(other, NC), lax.rem(other, NC)

    def q_dev(i):
        yy, cc = q_peer(i)
        return device(x, yy, z, cc)

    loop(NZ - 1, lambda i: greet(device(x, y, ring(z, i, NZ), c)))
    loop(NX - 1, lambda i: greet(device(ring(x, i, NX), y, z, c)))
    loop(NY * NC - 1, lambda i: greet(q_dev(i)))
    pl.semaphore_wait(barrier, NZ - 1 + NX - 1 + NY * NC - 1)

    pairs = ((dK, rk), (dV, rv))

    def k_copy(a, i, frm, to):
        src, dst = pairs[a]
        return remote(src.at[:, to], dst.at[frm], k_send.at[a, i], k_recv.at[a, frm], device(to, y, z, c))

    def q_copy(i, frm):
        yy, cc = q_peer(i)
        return remote(dQ.at[:, cc, yy], rq.at[frm], q_send.at[i], q_recv.at[frm], device(x, yy, z, cc))

    me = y * NC + c
    for a in range(2):
        for i in range(NX - 1):
            k_copy(a, i, x, ring(x, i, NX)).start()
    loop(NY * NC - 1, lambda i: q_copy(i, me).start())
    own_k = [pltpu.make_async_copy(pairs[a][0].at[:, x], pairs[a][1].at[x], own.at[a]) for a in range(2)]
    own_q = pltpu.make_async_copy(dQ.at[:, c, y], rq.at[me], own.at[2])
    for copy in (*own_k, own_q):
        copy.start()

    outs = (ok, ov, oq)

    def z_copy(a, i):
        to = ring(z, i, NZ)
        return remote(
            res.at[a, to], outs[a].at[:, columns(z)], z_send.at[a, i], z_recv.at[a, z],
            device(x, y, to, c),
        )

    def home(a):
        return pltpu.make_async_copy(res.at[a, z], outs[a].at[:, columns(z)], own.at[3 + a])

    def send_home(a):
        home(a).start()
        loop(NZ - 1, lambda i: z_copy(a, i).start())

    scale = DH**-0.5
    for a in range(2):
        for i in range(NX - 1):
            k_copy(a, i, ring(x, i, NX), x).wait_recv()
        own_k[a].wait()
        landed = pairs[a][1]

        def add_keys(zz, a=a, landed=landed):
            total = landed[0, zz].astype(F32)
            for xx in range(1, NX):
                total += landed[xx, zz].astype(F32)
            res[a, zz] = (total * scale if a == 0 else total).astype(BF16)

        loop(NZ, add_keys)
        send_home(a)

    loop(NY * NC - 1, lambda i: q_copy(i, lax.rem(me + i + 1, NY * NC)).wait_recv())
    own_q.wait()

    def add_queries(zz):
        total = rq[0, zz].astype(F32)
        for src in range(1, NY * NC):
            total += rq[src, zz].astype(F32)
        res[2, zz] = (total * scale).astype(BF16)

    loop(NZ, add_queries)
    send_home(2)

    for a in range(3):
        home(a).wait()

        def one(i, a=a):
            frm = ring(z, i, NZ)
            remote(
                res.at[a, frm], outs[a].at[:, columns(frm)], z_send.at[a, i], z_recv.at[a, frm],
                device(x, y, frm, c),
            ).wait_recv()

        loop(NZ - 1, one)

    for a in range(2):
        for i in range(NX - 1):
            k_copy(a, i, x, ring(x, i, NX)).wait_send()
    loop(NY * NC - 1, lambda i: q_copy(i, me).wait_send())
    for a in range(3):
        loop(NZ - 1, lambda i, a=a: z_copy(a, i).wait_send())


def return_grads(dQ, dK, dV):
    dma = pltpu.SemaphoreType.DMA
    hbm = pl.BlockSpec(memory_space=pl.ANY)
    out = jax.ShapeDtypeStruct((ROWS, NZ * DH), BF16)
    return pl.pallas_call(
        return_kernel,
        out_shape=(out, out, out),
        in_specs=[hbm] * 3,
        out_specs=(hbm,) * 3,
        scratch_shapes=[
            pltpu.VMEM((NY * NC, NZ, ROWS, DH), BF16),
            pltpu.VMEM((NX, NZ, ROWS, DH), BF16),
            pltpu.VMEM((NX, NZ, ROWS, DH), BF16),
            pltpu.VMEM((3, NZ, ROWS, DH), BF16),
            dma((NY * NC - 1,)), dma((NY * NC,)), dma((2, NX - 1)), dma((2, NX)), dma((6,)),
            dma((3, NZ - 1)), dma((3, NZ)),
        ],
        compiler_params=pltpu.CompilerParams(
            collective_id=1, has_side_effects=True, vmem_limit_bytes=32 * 1024 * 1024
        ),
        name="return_grads",
    )(dQ, dK, dV)


def per_device(queries, keys, values, outputs, grad_out, log_sums, doc_ids):
    landed = gather_inputs(
        queries, keys, values, outputs, grad_out, log_sums, doc_ids.reshape(1, CTX_ROWS)
    )
    return return_grads(*tile_grads(*landed))


def solution(mesh):
    tokens = P(("ctx", "head"), None)
    return jax.shard_map(
        per_device,
        mesh=mesh,
        in_specs=(tokens,) * 5 + (P("head", "ctx"), P("ctx")),
        out_specs=(tokens,) * 3,
        check_vma=False,
    )
```

time: 390 us -> 121 us (0.31)
  blocking collectives: 145 us -> 0 us
  waiting for transfers between devices: 124 us -> 0 us
  Pallas kernels: 0 us -> 110 us
  matrix products: 69.4 us -> 0 us
  starting transfers between devices: 20.4 us -> 0 us
  between operations: 13.8 us -> 0.67 us
  other arithmetic: 5.54 us -> 0 us
    all_gather x4 -> x0, waiting for transfers between devices: 113 us -> none  [the longest x1 72 us: per_device(): lax.all_gather(grad_rows, 'ctx', axis=0, tiled=True)]
    pallas_call x0 -> x3, Pallas kernels: none -> 110 us  [the longest x1 56.2 us: gather_inputs(): pl.pallas_call(gather_kernel, out_shape=(qg, kv, kv, qg, jax.ShapeDtypeSt...]
    all_gather x3 -> x0, blocking collectives: 102 us -> none  [the longest x1 42.2 us: per_device(): all_docs = lax.all_gather(doc_ids, 'ctx', axis=0, tiled=True)]
    dot_general x5 -> x0, matrix products: 69.4 us -> none  [the longest x2 26.6 us: contract_rows(): lax.dot_general(left, right, (((0,), (0,)), ((), ())), preferred_element_...]
    all_to_all x4 -> x0, blocking collectives: 43.6 us -> none  [the longest x1 14.1 us: per_device(): lax.all_to_all(keys, 'head', split_axis=1, concat_axis=0, tiled=True)]
    all_to_all x4 -> x0, starting transfers between devices: 20.3 us -> none  [the longest x1 6.7 us: per_device(): lax.all_to_all(grad_q, 'head', split_axis=0, concat_axis=1, tiled=True)]
    all_to_all x4 -> x0, waiting for transfers between devices: 11 us -> none  [the longest x1 5.95 us: per_device(): lax.all_to_all(grad_v, 'head', split_axis=0, concat_axis=1, tiled=True)]
    all_to_all x8 -> x0, local copies, waits for them, and re-layouts: 7.15 us -> none  [the longest x1 1.55 us: per_device(): lax.all_to_all(outputs, 'head', split_axis=1, concat_axis=0, tiled=True)]
  transfers between devices with their start and end apart: 8 -> 0, of which waited for: 5 -> 0; matrix products, arithmetic and copies ran while one was open for 21% -> 0% of each run, Pallas kernels for 0% -> 0%
where the time goes in v1:
time: 121 us; the launch traced here: 120 us
  Pallas kernels  110 us (91%)
  local copies, waits for them, and re-layouts  9.85 us (8%)
    pallas_call x1, Pallas kernels, gather_inputs(): pl.pallas_call(gather_kernel, out_shape=(qg, kv, kv, qg, jax.ShapeDtypeSt...  56.2 us
    pallas_call x1, Pallas kernels, return_grads(): pl.pallas_call(return_kernel, out_shape=(out, out, out), in_specs=[hbm] *...  33.7 us
    pallas_call x1, Pallas kernels, tile_grads(): pl.pallas_call(tile_kernel, out_shape=(qg, kv, kv), in_specs=[vmem] * 7,...  20 us
    unnamed x17, local copies, waits for them, and re-layouts  8.61 us

profile of v1, /device:TPU:1, one launch (start us, length us, event | category | flops | bytes accessed | tf_op | source)
XLA Modules:
  0.0 120.4 jit_solution(4261387530885427712)
XLA Ops:
  0.6 1.2 %reshape.9.doc = s32[1,384]{1,0:T(1,128)} reshape(s32[384]{0:T(512)} %param.13) | data formatting | bytes 3072 | tf_op jit(solution)/shard_map/reshape | solution.py:548
  1.9 56.2 %gather_inputs.1 = (bf16[16,2,4,24,128]{4,3,2,1,0:T(8,128)(2,1)}, bf16[16,4,24,128]{3,2,1,0:T(8,128)(2,1)}, bf16[16,4,24,128]{3,2,1,0:T(8,128)(2,1)}, bf16[16,2,...) custom-call(bf16[24,2048]{1,0:T(8,128)(2,1)} %q.1, ...), custom_call_target="tpu_custom_call" | custom-call | tf_op jit(solution)/shard_map/gather_inputs/pallas_call | solution.py:272
  58.1 0.0 copy-start
  58.1 1.1 copy-done
  59.3 0.0 copy-start.1
  59.3 1.1 copy-done.1
  60.4 0.0 copy-start.2
  60.4 1.0 copy-done.2
  61.4 0.0 copy-start.3
  61.4 1.0 copy-done.3
  62.4 0.0 copy-start.4
  62.4 0.8 copy-done.4
  63.2 0.0 copy-start.5
  63.2 0.8 copy-done.5
  64.0 0.0 copy-start.6
  64.0 0.8 copy-done.6
  64.8 20.0 %tile_grads.1 = (bf16[16,2,4,24,128]{4,3,2,1,0:T(8,128)(2,1)S(1)}, bf16[16,4,24,128]{3,2,1,0:T(8,128)(2,1)S(1)}, bf16[16,4,24,128]{3,2,1,0:T(8,128)(2,1)S(1)}) custom-call(bf16[16,2,4,24,128]{4,3,2,1,0:T(8,128)(2,1)S(1)} %copy-done, bf16[16,4,24,128]{3,2,1,0:T(8,128)(2,1)S(1)} %copy-done.2, bf16[16,4,24,128]{3,2,1,0:T(8,128)(2,1)S(1)} %copy-done.3, ...), custom_call_target="tpu_custom_call" | custom-call | tf_op jit(solution)/shard_map/tile_grads/pallas_call | solution.py:397
  84.8 33.7 %return_grads.1 = (bf16[24,2048]{1,0:T(8,128)(2,1)S(1)}, bf16[24,2048]{1,0:T(8,128)(2,1)S(1)}, bf16[24,2048]{1,0:T(8,128)(2,1)S(1)}) custom-call(bf16[16,2,4,24,128]{4,3,2,1,0:T(8,128)(2,1)S(1)} %get-tuple-element.20.dQ, bf16[16,4,24,128]{3,2,1,0:T(8,128)(2,1)S(1)} %get-tuple-element.21.dK, bf16[16,4,24,128]{3,2,1,0:T(8,128)(2,1)S(1)} %get-tuple-element.22.dV), custom_call_target="tpu_custom_call" | custom-call | tf_op jit(solution)/shard_map/return_grads/pallas_call | solution.py:526
  118.5 0.6 copy.13
  119.1 0.6 copy.14
  119.7 0.6 copy.15
Async XLA Ops:
  58.1 1.1 copy-start
  59.3 1.1 copy-start.1
  60.4 1.0 copy-start.2
  61.4 1.0 copy-start.3
  62.4 0.8 copy-start.4
  63.2 0.8 copy-start.5
  64.0 0.8 copy-start.6

commit v2 on v0

v2 whole, which is shorter than its diff:
```python
import jax
import jax.numpy as jnp
from jax import lax
from jax.experimental import pallas as pl
from jax.experimental.pallas import tpu as pltpu
from jax.sharding import PartitionSpec as P

DH = 128
NX, NY, NZ, NC = 4, 4, 16, 2
ROWS = 24
CTX_ROWS = NX * NY * ROWS
SPAN = NC * CTX_ROWS
Q_Z = NC * NY * ROWS
K_Z = NX * ROWS
BLK = 4
N_BLK = NZ // BLK
Q_BLK = BLK * Q_Z
K_BLK = BLK * K_Z
PART = NY * ROWS
MESH = pl.DeviceIdType.MESH
F32 = jnp.float32
BF16 = jnp.bfloat16


def here():
    ctx, head = lax.axis_index("ctx"), lax.axis_index("head")
    return lax.div(head, NY), lax.rem(head, NY), lax.div(ctx, NC), lax.rem(ctx, NC)


def device(x, y, z, c):
    return (z * NC + c, x * NY + y)


def ring(me, step, size):
    away = lax.div(step, 2) + 1
    return lax.rem(jnp.where(lax.rem(step, 2) == 0, me + away, me - away + size), size)


def columns(head):
    return pl.ds(pl.multiple_of(head * DH, DH), DH)


def remote(src, dst, send, recv, to):
    return pltpu.make_async_remote_copy(
        src_ref=src, dst_ref=dst, send_sem=send, recv_sem=recv, device_id=to, device_id_type=MESH
    )


def loop(count, body):
    def step(i, carry):
        body(i)
        return carry

    lax.fori_loop(0, count, step, 0)


def contract_last(left, right):
    return lax.dot_general(left, right, (((1,), (1,)), ((), ())), preferred_element_type=F32)


def block(i, size):
    return slice(i * size, (i + 1) * size)


def kernel(
    q, k, v, o, g, lse, doc,
    oq, ok, ov,
    Q, K, V, G, L, D, C, delta, docs,
    qs, ks, vs, gs, kt, probs, lse_s, delta_s,
    dq, dk, dv, rq, rk, rv, res,
    z_send, z_recv, own, d_send, d_recv, c_send, c_recv,
    hub_send, hub_recv, plane_send, plane_recv,
    x_send, x_recv, y_send, y_recv, s_send, s_recv,
    q_send, q_recv, k_send, k_recv, v_send, v_recv, h_send, h_recv,
):
    x, y, z, c = here()
    plane = x * NY + y
    sib = device(x, y, z, 1 - c)
    hub = z == plane
    scale = DH**-0.5

    barrier = pltpu.get_barrier_semaphore()

    def greet(to):
        pl.semaphore_signal(barrier, inc=1, device_id=to, device_id_type=MESH)

    def plane_peer(i):
        other = lax.rem(plane + i + 1, NX * NY)
        return device(lax.div(other, NY), lax.rem(other, NY), z, c)

    def q_peer(i):
        other = lax.rem(y * NC + c + i + 1, NY * NC)
        return lax.div(other, NC), lax.rem(other, NC)

    def q_dev(i):
        yy, cc = q_peer(i)
        return device(x, yy, z, cc)

    loop(NZ - 1, lambda i: greet(device(x, y, ring(z, i, NZ), c)))
    loop(NX - 1, lambda i: greet(device(ring(x, i, NX), y, z, c)))
    loop(NY * NC - 1, lambda i: greet(q_dev(i)))

    @pl.when(hub)
    def _():
        loop(NX * NY - 1, lambda i: greet(plane_peer(i)))

    @pl.when(jnp.logical_not(hub))
    def _():
        greet(device(lax.div(z, NY), lax.rem(z, NY), z, c))

    docs[...] = doc[...].reshape(1, CTX_ROWS)
    pl.semaphore_wait(
        barrier, NZ - 1 + NX - 1 + NY * NC - 1 + jnp.where(hub, NX * NY - 1, 1)
    )

    def doc_copy(i, frm):
        return remote(docs, C.at[c, frm], c_send.at[i], c_recv.at[frm], device(x, y, ring(z, i, NZ), c))

    def lse_copy(frm):
        return remote(lse, L.at[c, frm], hub_send, hub_recv.at[frm], device(x, y, plane, c))

    doc_own = pltpu.make_async_copy(docs, C.at[c, z], own.at[5])
    lse_own = pltpu.make_async_copy(lse, L.at[c, z], own.at[4])

    @pl.when(hub)
    def _():
        lse_own.start()

    @pl.when(jnp.logical_not(hub))
    def _():
        lse_copy(z).start()

    doc_own.start()
    loop(NZ - 1, lambda i: doc_copy(i, z).start())

    srcs = (q, k, g, v)

    def landing(a, zs):
        return (Q.at[zs, c, y], K.at[zs, x], G.at[zs, c, y], V.at[zs, x])[a]

    def z_copy(a, i):
        to = ring(z, i, NZ)
        return remote(
            srcs[a].at[:, columns(to)], landing(a, z), z_send.at[a, i], z_recv.at[a, z],
            device(x, y, to, c),
        )

    def own_copy(a):
        return pltpu.make_async_copy(srcs[a].at[:, columns(z)], landing(a, z), own.at[a])

    for a in range(4):
        own_copy(a).start()
        loop(NZ - 1, lambda i, a=a: z_copy(a, i).start())

    def z_wait(a):
        own_copy(a).wait()

        def one(i):
            frm = ring(z, i, NZ)
            remote(
                srcs[a].at[:, columns(frm)], landing(a, frm), z_send.at[a, i], z_recv.at[a, frm],
                device(x, y, frm, c),
            ).wait_recv()

        loop(NZ - 1, one)

    lane = lax.broadcasted_iota(jnp.int32, (ROWS, DH), 1)
    sums = jnp.zeros((ROWS, DH), F32)
    for h in range(NZ):
        cols = block(h, DH)
        row = jnp.sum(g[:, cols].astype(F32) * o[:, cols].astype(F32), axis=1, keepdims=True)
        sums = jnp.where(lane == h, row, sums)
    turned = jnp.concatenate([sums, jnp.zeros((DH - ROWS, DH), F32)], axis=0).T
    for h in range(NZ):
        delta[h] = turned[h : h + 1, :]

    def delta_copy(i, to, frm):
        return remote(
            delta.at[to], D.at[frm, c, y], d_send.at[i], d_recv.at[frm], device(x, y, ring(z, i, NZ), c)
        )

    delta_own = pltpu.make_async_copy(delta.at[z], D.at[z, c, y], own.at[6])
    delta_own.start()
    loop(NZ - 1, lambda i: delta_copy(i, ring(z, i, NZ), z).start())

    def sib_copy(part, slot):
        return remote(part, part, s_send.at[slot], s_recv.at[slot], sib)

    ys = (Q, G, D)

    def y_copy(a, i, frm, to):
        part = ys[a].at[:, c, frm]
        return remote(part, part, y_send.at[a, i], y_recv.at[a, frm], device(x, to, z, c))

    def sib_y(a, frm, core):
        return sib_copy(ys[a].at[:, core, frm], a * NY + frm)

    def y_start(a):
        for i in range(NY - 1):
            y_copy(a, i, y, ring(y, i, NY)).start()
        sib_y(a, y, c).start()

    def y_relay(a):
        for i in range(NY - 1):
            frm = ring(y, i, NY)
            y_copy(a, i, frm, y).wait_recv()
            sib_y(a, frm, c).start()

    def y_wait(a):
        for frm in range(NY):
            sib_y(a, frm, 1 - c).wait_recv()

    def x_copy(a, i, frm, to):
        part = (K, V)[a].at[:, frm]
        return remote(part, part, x_send.at[a, i], x_recv.at[a, frm], device(to, y, z, c))

    def x_start(a):
        for i in range(NX - 1):
            x_copy(a, i, x, ring(x, i, NX)).start()

    def x_wait(a):
        for i in range(NX - 1):
            x_copy(a, i, ring(x, i, NX), x).wait_recv()

    def plane_copy(i):
        return remote(L.at[c], L.at[c], plane_send.at[i], plane_recv, plane_peer(i))

    def doc_sib(core):
        return sib_copy(C.at[core], 3 * NY)

    def lse_sib(core):
        return sib_copy(L.at[core], 3 * NY + 1)

    @pl.when(hub)
    def _():
        lse_own.wait()

        def one(i):
            lse_copy(ring(z, i, NZ)).wait_recv()

        loop(NZ - 1, one)
        loop(NX * NY - 1, lambda i: plane_copy(i).start())

    doc_own.wait()
    loop(NZ - 1, lambda i: doc_copy(i, ring(z, i, NZ)).wait_recv())
    doc_sib(c).start()

    z_wait(0)
    y_start(0)

    @pl.when(jnp.logical_not(hub))
    def _():
        plane_copy(0).wait_recv()

    lse_sib(c).start()
    z_wait(1)
    x_start(0)
    y_relay(0)
    lse_sib(1 - c).wait_recv()
    doc_sib(1 - c).wait_recv()
    ends = [jnp.sum((C[...] < d).astype(jnp.int32)) for d in (1, 2, 3)]

    def doc_start(pos):
        start = jnp.where(pos >= ends[0], ends[0], 0)
        start = jnp.where(pos >= ends[1], ends[1], start)
        return jnp.where(pos >= ends[2], ends[2], start)

    def lay_rows(by_plane, out):
        for j in range(N_BLK):
            out[j] = jnp.concatenate([by_plane[zz : zz + 1] for zz in range(BLK * j, BLK * (j + 1))], axis=1)

    parts = []
    for core in range(NC):
        mine = jnp.concatenate([L[core, zz] for zz in range(NZ)], axis=0)
        picked = mine[:, :PART]
        for xx in range(1, NX):
            picked = jnp.where(x == xx, mine[:, block(xx, PART)], picked)
        parts.append(picked)
    lay_rows(jnp.concatenate(parts, axis=1), lse_s)

    q_at = lax.broadcasted_iota(jnp.int32, (1, Q_BLK), 1)
    q_in = lax.rem(q_at, Q_Z)
    q_base = (
        lax.div(q_at, Q_Z) * SPAN + lax.div(q_in, PART) * CTX_ROWS + x * PART + lax.rem(q_in, PART)
    )
    k_at = lax.broadcasted_iota(jnp.int32, (K_BLK, 1), 0)
    k_in = lax.rem(k_at, K_Z)
    k_base = (
        lax.div(k_at, K_Z) * SPAN
        + c * CTX_ROWS
        + lax.div(k_in, ROWS) * PART
        + y * ROWS
        + lax.rem(k_in, ROWS)
    )

    def flat(src, out, rows):
        def step(zz):
            at = pl.ds(pl.multiple_of(zz * rows, rows), rows)
            out[at, :] = src[zz].astype(F32).reshape(rows, DH).astype(BF16)

        loop(NZ, step)

    z_wait(2)
    y_start(1)
    y_wait(0)
    flat(Q, qs, Q_Z)
    x_wait(0)
    flat(K, ks, K_Z)

    def probs_block(j):
        q_pos = q_base + j * (BLK * SPAN)
        start = doc_start(q_pos)
        for i in range(j + 1):
            k_pos = k_base + i * (BLK * SPAN)
            allowed = jnp.where(k_pos < ends[0], NZ * SPAN, k_pos) >= start
            if i == j:
                allowed = allowed & (k_pos <= q_pos)
            s = contract_last(ks[block(i, K_BLK), :], qs[block(j, Q_BLK), :])
            p = jnp.where(allowed, jnp.exp(s * scale - lse_s[j]), 0.0)
            probs[block(i, K_BLK), block(j, Q_BLK)] = p.astype(BF16)

    probs_block(0)
    probs_block(1)
    z_wait(3)
    x_start(1)
    y_relay(1)
    probs_block(2)
    probs_block(3)

    y_wait(1)
    flat(G, gs, Q_Z)

    def v_copy(i, frm, to):
        return remote(dv.at[:, to], rv.at[frm], v_send.at[i], v_recv.at[frm], device(to, y, z, c))

    for i in range(N_BLK):
        total = jnp.dot(
            probs[block(i, K_BLK), i * Q_BLK :], gs[i * Q_BLK :, :], preferred_element_type=F32
        )
        dv[BLK * i : BLK * (i + 1)] = total.reshape(BLK, NX, ROWS, DH).astype(BF16)
    for i in range(NX - 1):
        v_copy(i, x, ring(x, i, NX)).start()

    delta_own.wait()
    loop(NZ - 1, lambda i: delta_copy(i, z, ring(z, i, NZ)).wait_recv())
    y_start(2)
    y_relay(2)
    for i in range(N_BLK):
        kt[i] = ks[block(i, K_BLK), :].T
    y_wait(2)
    parts = []
    for core in range(NC):
        for yy in range(NY):
            rows = jnp.concatenate([D[zz, core, yy] for zz in range(NZ)], axis=0)
            parts.append(rows[:, :ROWS])
    lay_rows(jnp.concatenate(parts, axis=1), delta_s)
    x_wait(1)
    flat(V, vs, K_Z)

    me = y * NC + c

    def k_copy(j, i, frm, to):
        rows = pl.ds(BLK * j, BLK)
        return remote(
            dk.at[rows, to], rk.at[frm, rows], k_send.at[j, i], k_recv.at[j, frm], device(to, y, z, c)
        )

    def q_copy(j, i, frm):
        rows = pl.ds(BLK * j, BLK)
        yy, cc = q_peer(i)
        return remote(
            dq.at[rows, cc, yy], rq.at[frm, rows], q_send.at[j, i], q_recv.at[j, frm],
            device(x, yy, z, cc),
        )

    def grads_block(j):
        total = jnp.zeros((DH, Q_BLK), F32)
        for i in range(j + 1):
            dp = contract_last(vs[block(i, K_BLK), :], gs[block(j, Q_BLK), :])
            p = probs[block(i, K_BLK), block(j, Q_BLK)].astype(F32)
            ds = (p * (dp - delta_s[j])).astype(BF16)
            probs[block(i, K_BLK), block(j, Q_BLK)] = ds
            total += jnp.dot(kt[i], ds, preferred_element_type=F32)
        dq[BLK * j : BLK * (j + 1)] = total.T.reshape(BLK, NC, NY, ROWS, DH).astype(BF16)
        loop(NY * NC - 1, lambda i: q_copy(j, i, me).start())
        total = jnp.dot(
            probs[block(j, K_BLK), j * Q_BLK :], qs[j * Q_BLK :, :], preferred_element_type=F32
        )
        dk[BLK * j : BLK * (j + 1)] = total.reshape(BLK, NX, ROWS, DH).astype(BF16)
        for i in range(NX - 1):
            k_copy(j, i, x, ring(x, i, NX)).start()

    outs = (oq, ok, ov)

    def home_copy(a, to, frm):
        return remote(
            res.at[a, to], outs[a].at[:, columns(frm)], h_send.at[a, to], h_recv.at[a, frm],
            device(x, y, to, c),
        )

    def home_own(a):
        return pltpu.make_async_copy(res.at[a, z], outs[a].at[:, columns(z)], own.at[7 + a])

    def send_home(a, to):
        @pl.when(to == z)
        def _():
            home_own(a).start()

        @pl.when(to != z)
        def _():
            home_copy(a, to, z).start()

    def add_v():
        for i in range(NX - 1):
            v_copy(i, ring(x, i, NX), x).wait_recv()

        def one(zz):
            total = dv[zz, x].astype(F32)
            for i in range(NX - 1):
                total += rv[ring(x, i, NX), zz].astype(F32)
            res[2, zz] = total.astype(BF16)

        loop(NZ, one)
        loop(NZ, lambda i: send_home(2, lax.rem(z + i, NZ)))

    def add_block(j):
        for i in range(NX - 1):
            k_copy(j, i, ring(x, i, NX), x).wait_recv()
        loop(NY * NC - 1, lambda i: q_copy(j, i, lax.rem(me + i + 1, NY * NC)).wait_recv())

        def one(step):
            zz = BLK * j + step
            total = dk[zz, x].astype(F32)
            for i in range(NX - 1):
                total += rk[ring(x, i, NX), zz].astype(F32)
            res[1, zz] = (total * scale).astype(BF16)
            total = dq[zz, c, y].astype(F32)
            for i in range(NY * NC - 1):
                total += rq[lax.rem(me + i + 1, NY * NC), zz].astype(F32)
            res[0, zz] = (total * scale).astype(BF16)
            send_home(1, zz)
            send_home(0, zz)

        loop(BLK, one)

    grads_block(3)
    add_v()
    grads_block(2)
    add_block(3)
    grads_block(1)
    add_block(2)
    grads_block(0)
    add_block(1)
    add_block(0)

    for a in range(4):
        loop(NZ - 1, lambda i, a=a: z_copy(a, i).wait_send())
    loop(NZ - 1, lambda i: doc_copy(i, z).wait_send())
    loop(NZ - 1, lambda i: delta_copy(i, ring(z, i, NZ), z).wait_send())

    @pl.when(jnp.logical_not(hub))
    def _():
        lse_copy(z).wait_send()

    @pl.when(hub)
    def _():
        loop(NX * NY - 1, lambda i: plane_copy(i).wait_send())

    for a in range(2):
        for i in range(NX - 1):
            x_copy(a, i, x, ring(x, i, NX)).wait_send()
    for a in range(3):
        for i in range(NY - 1):
            y_copy(a, i, y, ring(y, i, NY)).wait_send()
        for frm in range(NY):
            sib_y(a, frm, c).wait_send()
    doc_sib(c).wait_send()
    lse_sib(c).wait_send()
    for i in range(NX - 1):
        v_copy(i, x, ring(x, i, NX)).wait_send()
    for j in range(N_BLK):
        for i in range(NX - 1):
            k_copy(j, i, x, ring(x, i, NX)).wait_send()
        loop(NY * NC - 1, lambda i, j=j: q_copy(j, i, me).wait_send())
    for a in range(3):
        home_own(a).wait()

        def one(i, a=a):
            peer = ring(z, i, NZ)
            home_copy(a, peer, z).wait_send()
            home_copy(a, z, peer).wait_recv()

        loop(NZ - 1, one)


def per_device(queries, keys, values, outputs, grad_out, log_sums, doc_ids):
    dma = pltpu.SemaphoreType.DMA
    vmem = pl.BlockSpec(memory_space=pltpu.VMEM)
    hbm = pl.BlockSpec(memory_space=pl.ANY)
    out = jax.ShapeDtypeStruct((ROWS, NZ * DH), BF16)
    kv, qg = (NZ, NX, ROWS, DH), (NZ, NC, NY, ROWS, DH)
    return pl.pallas_call(
        kernel,
        out_shape=(out, out, out),
        in_specs=[vmem] * 7,
        out_specs=(hbm,) * 3,
        scratch_shapes=[
            pltpu.VMEM(qg, BF16), pltpu.VMEM(kv, BF16), pltpu.VMEM(kv, BF16), pltpu.VMEM(qg, BF16),
            pltpu.VMEM((NC, NZ, 1, CTX_ROWS), F32),
            pltpu.VMEM((NZ, NC, NY, 1, DH), F32),
            pltpu.VMEM((NC, NZ, 1, CTX_ROWS), jnp.int32),
            pltpu.VMEM((NZ, 1, DH), F32), pltpu.VMEM((1, CTX_ROWS), jnp.int32),
            pltpu.VMEM((NZ * Q_Z, DH), BF16), pltpu.VMEM((NZ * K_Z, DH), BF16),
            pltpu.VMEM((NZ * K_Z, DH), BF16), pltpu.VMEM((NZ * Q_Z, DH), BF16),
            pltpu.VMEM((N_BLK, DH, K_BLK), BF16), pltpu.VMEM((NZ * K_Z, NZ * Q_Z), BF16),
            pltpu.VMEM((N_BLK, 1, Q_BLK), F32), pltpu.VMEM((N_BLK, 1, Q_BLK), F32),
            pltpu.VMEM(qg, BF16), pltpu.VMEM(kv, BF16), pltpu.VMEM(kv, BF16),
            pltpu.VMEM((NY * NC, NZ, ROWS, DH), BF16),
            pltpu.VMEM((NX, NZ, ROWS, DH), BF16), pltpu.VMEM((NX, NZ, ROWS, DH), BF16),
            pltpu.VMEM((3, NZ, ROWS, DH), BF16),
            dma((4, NZ - 1)), dma((4, NZ)), dma((10,)),
            dma((NZ - 1,)), dma((NZ,)), dma((NZ - 1,)), dma((NZ,)),
            dma, dma((NZ,)), dma((NX * NY - 1,)), dma,
            dma((2, NX - 1)), dma((2, NX)), dma((3, NY - 1)), dma((3, NY)),
            dma((3 * NY + 2,)), dma((3 * NY + 2,)),
            dma((N_BLK, NY * NC - 1)), dma((N_BLK, NY * NC)), dma((N_BLK, NX - 1)), dma((N_BLK, NX)),
            dma((NX - 1,)), dma((NX,)), dma((3, NZ)), dma((3, NZ)),
        ],
        compiler_params=pltpu.CompilerParams(
            collective_id=0, has_side_effects=True, vmem_limit_bytes=50 * 1024 * 1024
        ),
        name="attention_grads",
    )(queries, keys, values, outputs, grad_out, log_sums, doc_ids)


def solution(mesh):
    tokens = P(("ctx", "head"), None)
    return jax.shard_map(
        per_device,
        mesh=mesh,
        in_specs=(tokens,) * 5 + (P("head", "ctx"), P("ctx")),
        out_specs=(tokens,) * 3,
        check_vma=False,
    )
```

time: 390 us -> 91.4 us (0.23)
  the two profiles are of different devices: /device:TPU:1 before, /device:TPU:33 now
where the time goes in v2:
time: 91.4 us; the launch traced here: 91.1 us
  Pallas kernels  82.7 us (90%)
  local copies, waits for them, and re-layouts  7.74 us (8%)
    pallas_call x1, Pallas kernels, per_device(): pl.pallas_call(kernel, out_shape=(out, out, out), in_specs=[vmem] * 7, ou...  82.7 us
    unnamed x17, local copies, waits for them, and re-layouts  7.74 us

profile of v2, /device:TPU:33, one launch (start us, length us, event | category | flops | bytes accessed | tf_op | source)
XLA Modules:
  0.0 91.1 jit_solution(14153721938906332542)
XLA Ops:
  0.6 0.0 copy-start
  0.6 0.9 copy-done
  1.5 0.0 copy-start.1
  1.5 0.9 copy-done.1
  2.4 0.0 copy-start.2
  2.4 0.9 copy-done.2
  3.3 0.0 copy-start.3
  3.3 0.9 copy-done.3
  4.2 0.0 copy-start.4
  4.2 0.9 copy-done.4
  5.1 0.0 copy-start.5
  5.1 0.7 copy-done.5
  5.8 0.0 copy-start.6
  5.8 0.7 copy-done.6
  6.5 82.7 %attention_grads.1 = (bf16[24,2048]{1,0:T(8,128)(2,1)S(1)}, bf16[24,2048]{1,0:T(8,128)(2,1)S(1)}, bf16[24,2048]{1,0:T(8,128)(2,1)S(1)}) custom-call(bf16[24,2048]{1,0:T(8,128)(2,1)S(1)} %copy-done, bf16[24,2048]{1,0:T(8,128)(2,1)S(1)} %copy-done.1, bf16[24,2048]{1,0:T(8,128)(2,1)S(1)} %copy-done.2, bf16[24,2048]{1,0:T(8,128)(2,1)S(1)} %copy-done.3, ...), custom_call_target="tpu_custom_call" | custom-call | tf_op jit(solution)/shard_map/attention_grads/pallas_call | solution.py:502
  89.2 0.6 copy.13
  89.8 0.6 copy.14
  90.5 0.6 copy.15
Async XLA Ops:
  0.6 0.9 copy-start
  1.5 0.9 copy-start.1
  2.4 0.9 copy-start.2
  3.3 0.9 copy-start.3
  4.2 0.9 copy-start.4
  5.1 0.7 copy-start.5
  5.8 0.7 copy-start.6

commit v3 on v2

--- a/solution.py
+++ b/solution.py
@@ -17,6 +17,7 @@
 Q_BLK = BLK * Q_Z
 K_BLK = BLK * K_Z
 PART = NY * ROWS
+STATS = CTX_ROWS + DH
 MESH = pl.DeviceIdType.MESH
 F32 = jnp.float32
 BF16 = jnp.bfloat16
@@ -65,12 +66,13 @@
 def kernel(
     q, k, v, o, g, lse, doc,
     oq, ok, ov,
-    Q, K, V, G, L, D, C, delta, docs,
+    Q, K, V, G, L, D, delta, stats, doc_in, lse_in, g_in, o_in,
     qs, ks, vs, gs, kt, probs, lse_s, delta_s,
-    dq, dk, dv, rq, rk, rv, res,
-    z_send, z_recv, own, d_send, d_recv, c_send, c_recv,
+    dq, dk, dv, pq, rs, rq, rk, rv, res,
+    z_send, z_recv, own, d_send, d_recv,
     hub_send, hub_recv, plane_send, plane_recv,
     x_send, x_recv, y_send, y_recv, s_send, s_recv,
+    xv_send, xv_recv, p_send, p_recv,
     q_send, q_recv, k_send, k_recv, v_send, v_recv, h_send, h_recv,
 ):
     x, y, z, c = here()
@@ -88,17 +90,16 @@
         other = lax.rem(plane + i + 1, NX * NY)
         return device(lax.div(other, NY), lax.rem(other, NY), z, c)
 
-    def q_peer(i):
-        other = lax.rem(y * NC + c + i + 1, NY * NC)
-        return lax.div(other, NC), lax.rem(other, NC)
-
-    def q_dev(i):
-        yy, cc = q_peer(i)
-        return device(x, yy, z, cc)
-
     loop(NZ - 1, lambda i: greet(device(x, y, ring(z, i, NZ), c)))
+    fetch = [
+        pltpu.make_async_copy(src, dst, own.at[10 + i])
+        for i, (src, dst) in enumerate(((doc, doc_in), (lse, lse_in), (g, g_in), (o, o_in)))
+    ]
+    for copy in fetch:
+        copy.start()
     loop(NX - 1, lambda i: greet(device(ring(x, i, NX), y, z, c)))
-    loop(NY * NC - 1, lambda i: greet(q_dev(i)))
+    loop(NY - 1, lambda i: greet(device(x, ring(y, i, NY), z, c)))
+    greet(sib)
 
     @pl.when(hub)
     def _():
@@ -108,30 +109,14 @@
     def _():
         greet(device(lax.div(z, NY), lax.rem(z, NY), z, c))
 
-    docs[...] = doc[...].reshape(1, CTX_ROWS)
     pl.semaphore_wait(
-        barrier, NZ - 1 + NX - 1 + NY * NC - 1 + jnp.where(hub, NX * NY - 1, 1)
+        barrier, NZ - 1 + NX - 1 + NY - 1 + 1 + jnp.where(hub, NX * NY - 1, 1)
     )
 
-    def doc_copy(i, frm):
-        return remote(docs, C.at[c, frm], c_send.at[i], c_recv.at[frm], device(x, y, ring(z, i, NZ), c))
-
     def lse_copy(frm):
-        return remote(lse, L.at[c, frm], hub_send, hub_recv.at[frm], device(x, y, plane, c))
-
-    doc_own = pltpu.make_async_copy(docs, C.at[c, z], own.at[5])
-    lse_own = pltpu.make_async_copy(lse, L.at[c, z], own.at[4])
-
-    @pl.when(hub)
-    def _():
-        lse_own.start()
-
-    @pl.when(jnp.logical_not(hub))
-    def _():
-        lse_copy(z).start()
-
-    doc_own.start()
-    loop(NZ - 1, lambda i: doc_copy(i, z).start())
+        return remote(stats, L.at[c, frm], hub_send, hub_recv.at[frm], device(x, y, plane, c))
+
+    lse_own = pltpu.make_async_copy(stats, L.at[c, z], own.at[4])
 
     srcs = (q, k, g, v)
 
@@ -148,27 +133,51 @@
     def own_copy(a):
         return pltpu.make_async_copy(srcs[a].at[:, columns(z)], landing(a, z), own.at[a])
 
-    for a in range(4):
+    def z_start(a):
         own_copy(a).start()
-        loop(NZ - 1, lambda i, a=a: z_copy(a, i).start())
+        loop(NZ - 1, lambda i: z_copy(a, i).start())
+
+    def z_wait_from(a, i):
+        frm = ring(z, i, NZ)
+        remote(
+            srcs[a].at[:, columns(frm)], landing(a, frm), z_send.at[a, i], z_recv.at[a, frm],
+            device(x, y, frm, c),
+        ).wait_recv()
 
     def z_wait(a):
         own_copy(a).wait()
-
-        def one(i):
-            frm = ring(z, i, NZ)
-            remote(
-                srcs[a].at[:, columns(frm)], landing(a, frm), z_send.at[a, i], z_recv.at[a, frm],
-                device(x, y, frm, c),
-            ).wait_recv()
-
-        loop(NZ - 1, one)
+        loop(NZ - 1, lambda i: z_wait_from(a, i))
+
+    z_start(0)
+    z_start(1)
 
     lane = lax.broadcasted_iota(jnp.int32, (ROWS, DH), 1)
+    fetch[0].wait()
+    fetch[1].wait()
+    numbers = doc_in[...].reshape(1, CTX_ROWS)
+    counts = jnp.zeros((1, DH), F32)
+    for d in range(3):
+        before = jnp.sum((numbers <= d).astype(F32), axis=1, keepdims=True)
+        counts = jnp.where(lane[:1] == d, before, counts)
+    stats[...] = jnp.concatenate([lse_in[...], counts], axis=1)
+
+    @pl.when(hub)
+    def _():
+        lse_own.start()
+
+    @pl.when(jnp.logical_not(hub))
+    def _():
+        lse_copy(z).start()
+
+    z_start(2)
+    z_start(3)
+
+    fetch[2].wait()
+    fetch[3].wait()
     sums = jnp.zeros((ROWS, DH), F32)
     for h in range(NZ):
         cols = block(h, DH)
-        row = jnp.sum(g[:, cols].astype(F32) * o[:, cols].astype(F32), axis=1, keepdims=True)
+        row = jnp.sum(g_in[:, cols].astype(F32) * o_in[:, cols].astype(F32), axis=1, keepdims=True)
         sums = jnp.where(lane == h, row, sums)
     turned = jnp.concatenate([sums, jnp.zeros((DH - ROWS, DH), F32)], axis=0).T
     for h in range(NZ):
@@ -210,26 +219,30 @@
         for frm in range(NY):
             sib_y(a, frm, 1 - c).wait_recv()
 
-    def x_copy(a, i, frm, to):
-        part = (K, V)[a].at[:, frm]
-        return remote(part, part, x_send.at[a, i], x_recv.at[a, frm], device(to, y, z, c))
-
-    def x_start(a):
+    def x_copy(i, frm, to):
+        part = K.at[:, frm]
+        return remote(part, part, x_send.at[i], x_recv.at[frm], device(to, y, z, c))
+
+    def xv_copy(i, zs, frm, to):
+        part = V.at[zs, frm]
+        return remote(part, part, xv_send.at[i, zs], xv_recv.at[frm, zs], device(to, y, z, c))
+
+    def xv_start(zs):
         for i in range(NX - 1):
-            x_copy(a, i, x, ring(x, i, NX)).start()
-
-    def x_wait(a):
-        for i in range(NX - 1):
-            x_copy(a, i, ring(x, i, NX), x).wait_recv()
+            xv_copy(i, zs, x, ring(x, i, NX)).start()
+
+    def pass_values(first, last):
+        def one(i):
+            z_wait_from(3, first + i)
+            xv_start(ring(z, first + i, NZ))
+
+        loop(last - first, one)
 
     def plane_copy(i):
         return remote(L.at[c], L.at[c], plane_send.at[i], plane_recv, plane_peer(i))
 
-    def doc_sib(core):
-        return sib_copy(C.at[core], 3 * NY)
-
     def lse_sib(core):
-        return sib_copy(L.at[core], 3 * NY + 1)
+        return sib_copy(L.at[core], 3 * NY)
 
     @pl.when(hub)
     def _():
@@ -241,24 +254,27 @@
         loop(NZ - 1, one)
         loop(NX * NY - 1, lambda i: plane_copy(i).start())
 
-    doc_own.wait()
-    loop(NZ - 1, lambda i: doc_copy(i, ring(z, i, NZ)).wait_recv())
-    doc_sib(c).start()
-
     z_wait(0)
     y_start(0)
+    z_wait(1)
+    for i in range(NX - 1):
+        x_copy(i, x, ring(x, i, NX)).start()
 
     @pl.when(jnp.logical_not(hub))
     def _():
         plane_copy(0).wait_recv()
 
     lse_sib(c).start()
-    z_wait(1)
-    x_start(0)
+    z_wait(2)
+    y_start(1)
     y_relay(0)
+    delta_own.wait()
+    loop(NZ - 1, lambda i: delta_copy(i, z, ring(z, i, NZ)).wait_recv())
+    y_start(2)
     lse_sib(1 - c).wait_recv()
-    doc_sib(1 - c).wait_recv()
-    ends = [jnp.sum((C[...] < d).astype(jnp.int32)) for d in (1, 2, 3)]
+    rows = [jnp.concatenate([L[core, zz] for zz in range(NZ)], axis=0) for core in range(NC)]
+    counts = rows[0][:, CTX_ROWS:] + rows[1][:, CTX_ROWS:]
+    ends = [jnp.sum(counts[:, d : d + 1]).astype(jnp.int32) for d in range(3)]
 
     def doc_start(pos):
         start = jnp.where(pos >= ends[0], ends[0], 0)
@@ -271,10 +287,9 @@
 
     parts = []
     for core in range(NC):
-        mine = jnp.concatenate([L[core, zz] for zz in range(NZ)], axis=0)
-        picked = mine[:, :PART]
+        picked = rows[core][:, :PART]
         for xx in range(1, NX):
-            picked = jnp.where(x == xx, mine[:, block(xx, PART)], picked)
+            picked = jnp.where(x == xx, rows[core][:, block(xx, PART)], picked)
         parts.append(picked)
     lay_rows(jnp.concatenate(parts, axis=1), lse_s)
 
@@ -300,11 +315,10 @@
 
         loop(NZ, step)
 
-    z_wait(2)
-    y_start(1)
     y_wait(0)
     flat(Q, qs, Q_Z)
-    x_wait(0)
+    for i in range(NX - 1):
+        x_copy(i, ring(x, i, NX), x).wait_recv()
     flat(K, ks, K_Z)
 
     def probs_block(j):
@@ -321,11 +335,14 @@
 
     probs_block(0)
     probs_block(1)
-    z_wait(3)
-    x_start(1)
+    own_copy(3).wait()
+    xv_start(z)
+    pass_values(0, 8)
+    probs_block(2)
+    pass_values(8, NZ - 1)
     y_relay(1)
-    probs_block(2)
     probs_block(3)
+    y_relay(2)
 
     y_wait(1)
     flat(G, gs, Q_Z)
@@ -341,23 +358,17 @@
     for i in range(NX - 1):
         v_copy(i, x, ring(x, i, NX)).start()
 
-    delta_own.wait()
-    loop(NZ - 1, lambda i: delta_copy(i, z, ring(z, i, NZ)).wait_recv())
-    y_start(2)
-    y_relay(2)
-    for i in range(N_BLK):
-        kt[i] = ks[block(i, K_BLK), :].T
     y_wait(2)
     parts = []
     for core in range(NC):
         for yy in range(NY):
-            rows = jnp.concatenate([D[zz, core, yy] for zz in range(NZ)], axis=0)
-            parts.append(rows[:, :ROWS])
+            parts.append(jnp.concatenate([D[zz, core, yy] for zz in range(NZ)], axis=0)[:, :ROWS])
     lay_rows(jnp.concatenate(parts, axis=1), delta_s)
-    x_wait(1)
+    for i in range(N_BLK):
+        kt[i] = ks[block(i, K_BLK), :].T
+    for i in range(NX - 1):
+        loop(NZ, lambda zs, i=i: xv_copy(i, zs, ring(x, i, NX), x).wait_recv())
     flat(V, vs, K_Z)
-
-    me = y * NC + c
 
     def k_copy(j, i, frm, to):
         rows = pl.ds(BLK * j, BLK)
@@ -365,12 +376,14 @@
             dk.at[rows, to], rk.at[frm, rows], k_send.at[j, i], k_recv.at[j, frm], device(to, y, z, c)
         )
 
-    def q_copy(j, i, frm):
+    def p_copy(j, core):
         rows = pl.ds(BLK * j, BLK)
-        yy, cc = q_peer(i)
+        return remote(dq.at[rows, core], rs.at[rows], p_send.at[j], p_recv.at[j], sib)
+
+    def q_copy(j, i, frm, to):
+        rows = pl.ds(BLK * j, BLK)
         return remote(
-            dq.at[rows, cc, yy], rq.at[frm, rows], q_send.at[j, i], q_recv.at[j, frm],
-            device(x, yy, z, cc),
+            pq.at[rows, to], rq.at[frm, rows], q_send.at[j, i], q_recv.at[j, frm], device(x, to, z, c)
         )
 
     def grads_block(j):
@@ -382,7 +395,7 @@
             probs[block(i, K_BLK), block(j, Q_BLK)] = ds
             total += jnp.dot(kt[i], ds, preferred_element_type=F32)
         dq[BLK * j : BLK * (j + 1)] = total.T.reshape(BLK, NC, NY, ROWS, DH).astype(BF16)
-        loop(NY * NC - 1, lambda i: q_copy(j, i, me).start())
+        p_copy(j, 1 - c).start()
         total = jnp.dot(
             probs[block(j, K_BLK), j * Q_BLK :], qs[j * Q_BLK :, :], preferred_element_type=F32
         )
@@ -423,10 +436,22 @@
         loop(NZ, one)
         loop(NZ, lambda i: send_home(2, lax.rem(z + i, NZ)))
 
+    def pair_block(j):
+        p_copy(j, c).wait_recv()
+
+        def one(step):
+            zz = BLK * j + step
+            pq[zz] = (dq[zz, c].astype(F32) + rs[zz].astype(F32)).astype(BF16)
+
+        loop(BLK, one)
+        for i in range(NY - 1):
+            q_copy(j, i, y, ring(y, i, NY)).start()
+
     def add_block(j):
         for i in range(NX - 1):
             k_copy(j, i, ring(x, i, NX), x).wait_recv()
-        loop(NY * NC - 1, lambda i: q_copy(j, i, lax.rem(me + i + 1, NY * NC)).wait_recv())
+        for i in range(NY - 1):
+            q_copy(j, i, ring(y, i, NY), y).wait_recv()
 
         def one(step):
             zz = BLK * j + step
@@ -434,9 +459,9 @@
             for i in range(NX - 1):
                 total += rk[ring(x, i, NX), zz].astype(F32)
             res[1, zz] = (total * scale).astype(BF16)
-            total = dq[zz, c, y].astype(F32)
-            for i in range(NY * NC - 1):
-                total += rq[lax.rem(me + i + 1, NY * NC), zz].astype(F32)
+            total = pq[zz, y].astype(F32)
+            for i in range(NY - 1):
+                total += rq[ring(y, i, NY), zz].astype(F32)
             res[0, zz] = (total * scale).astype(BF16)
             send_home(1, zz)
             send_home(0, zz)
@@ -444,18 +469,21 @@
         loop(BLK, one)
 
     grads_block(3)
+    grads_block(2)
+    pair_block(3)
+    grads_block(1)
+    pair_block(2)
     add_v()
-    grads_block(2)
+    grads_block(0)
+    pair_block(1)
+    pair_block(0)
     add_block(3)
-    grads_block(1)
     add_block(2)
-    grads_block(0)
     add_block(1)
     add_block(0)
 
     for a in range(4):
         loop(NZ - 1, lambda i, a=a: z_copy(a, i).wait_send())
-    loop(NZ - 1, lambda i: doc_copy(i, z).wait_send())
     loop(NZ - 1, lambda i: delta_copy(i, ring(z, i, NZ), z).wait_send())
 
     @pl.when(jnp.logical_not(hub))
@@ -466,22 +494,23 @@
     def _():
         loop(NX * NY - 1, lambda i: plane_copy(i).wait_send())
 
-    for a in range(2):
-        for i in range(NX - 1):
-            x_copy(a, i, x, ring(x, i, NX)).wait_send()
+    for i in range(NX - 1):
+        x_copy(i, x, ring(x, i, NX)).wait_send()
+        loop(NZ, lambda zs, i=i: xv_copy(i, zs, x, ring(x, i, NX)).wait_send())
     for a in range(3):
         for i in range(NY - 1):
             y_copy(a, i, y, ring(y, i, NY)).wait_send()
         for frm in range(NY):
             sib_y(a, frm, c).wait_send()
-    doc_sib(c).wait_send()
     lse_sib(c).wait_send()
     for i in range(NX - 1):
         v_copy(i, x, ring(x, i, NX)).wait_send()
     for j in range(N_BLK):
         for i in range(NX - 1):
             k_copy(j, i, x, ring(x, i, NX)).wait_send()
-        loop(NY * NC - 1, lambda i, j=j: q_copy(j, i, me).wait_send())
+        for i in range(NY - 1):
+            q_copy(j, i, y, ring(y, i, NY)).wait_send()
+        p_copy(j, 1 - c).wait_send()
     for a in range(3):
         home_own(a).wait()
 
@@ -493,44 +522,58 @@
         loop(NZ - 1, one)
 
 
+def copy_kernel(a, b, c, out_a, out_b, out_c):
+    out_a[...], out_b[...], out_c[...] = a[...], b[...], c[...]
+
+
+def copied(grads):
+    vmem = pl.BlockSpec(memory_space=pltpu.VMEM)
+    out = jax.ShapeDtypeStruct((ROWS, NZ * DH), BF16)
+    return pl.pallas_call(
+        copy_kernel, out_shape=(out,) * 3, in_specs=[vmem] * 3, out_specs=(vmem,) * 3, name="copy_grads"
+    )(*grads)
+
+
 def per_device(queries, keys, values, outputs, grad_out, log_sums, doc_ids):
     dma = pltpu.SemaphoreType.DMA
-    vmem = pl.BlockSpec(memory_space=pltpu.VMEM)
     hbm = pl.BlockSpec(memory_space=pl.ANY)
     out = jax.ShapeDtypeStruct((ROWS, NZ * DH), BF16)
     kv, qg = (NZ, NX, ROWS, DH), (NZ, NC, NY, ROWS, DH)
-    return pl.pallas_call(
+    grads = pl.pallas_call(
         kernel,
         out_shape=(out, out, out),
-        in_specs=[vmem] * 7,
+        in_specs=[pl.BlockSpec(memory_space=pltpu.HBM)] * 7,
         out_specs=(hbm,) * 3,
         scratch_shapes=[
             pltpu.VMEM(qg, BF16), pltpu.VMEM(kv, BF16), pltpu.VMEM(kv, BF16), pltpu.VMEM(qg, BF16),
-            pltpu.VMEM((NC, NZ, 1, CTX_ROWS), F32),
+            pltpu.VMEM((NC, NZ, 1, STATS), F32),
             pltpu.VMEM((NZ, NC, NY, 1, DH), F32),
-            pltpu.VMEM((NC, NZ, 1, CTX_ROWS), jnp.int32),
-            pltpu.VMEM((NZ, 1, DH), F32), pltpu.VMEM((1, CTX_ROWS), jnp.int32),
+            pltpu.VMEM((NZ, 1, DH), F32), pltpu.VMEM((1, STATS), F32),
+            pltpu.VMEM((CTX_ROWS,), jnp.int32), pltpu.VMEM((1, CTX_ROWS), F32), pltpu.VMEM((ROWS, NZ * DH), BF16), pltpu.VMEM((ROWS, NZ * DH), BF16),
             pltpu.VMEM((NZ * Q_Z, DH), BF16), pltpu.VMEM((NZ * K_Z, DH), BF16),
             pltpu.VMEM((NZ * K_Z, DH), BF16), pltpu.VMEM((NZ * Q_Z, DH), BF16),
             pltpu.VMEM((N_BLK, DH, K_BLK), BF16), pltpu.VMEM((NZ * K_Z, NZ * Q_Z), BF16),
             pltpu.VMEM((N_BLK, 1, Q_BLK), F32), pltpu.VMEM((N_BLK, 1, Q_BLK), F32),
             pltpu.VMEM(qg, BF16), pltpu.VMEM(kv, BF16), pltpu.VMEM(kv, BF16),
-            pltpu.VMEM((NY * NC, NZ, ROWS, DH), BF16),
+            pltpu.VMEM((NZ, NY, ROWS, DH), BF16), pltpu.VMEM((NZ, NY, ROWS, DH), BF16),
+            pltpu.VMEM((NY, NZ, ROWS, DH), BF16),
             pltpu.VMEM((NX, NZ, ROWS, DH), BF16), pltpu.VMEM((NX, NZ, ROWS, DH), BF16),
             pltpu.VMEM((3, NZ, ROWS, DH), BF16),
-            dma((4, NZ - 1)), dma((4, NZ)), dma((10,)),
-            dma((NZ - 1,)), dma((NZ,)), dma((NZ - 1,)), dma((NZ,)),
+            dma((4, NZ - 1)), dma((4, NZ)), dma((14,)),
+            dma((NZ - 1,)), dma((NZ,)),
             dma, dma((NZ,)), dma((NX * NY - 1,)), dma,
-            dma((2, NX - 1)), dma((2, NX)), dma((3, NY - 1)), dma((3, NY)),
-            dma((3 * NY + 2,)), dma((3 * NY + 2,)),
-            dma((N_BLK, NY * NC - 1)), dma((N_BLK, NY * NC)), dma((N_BLK, NX - 1)), dma((N_BLK, NX)),
+            dma((NX - 1,)), dma((NX,)), dma((3, NY - 1)), dma((3, NY)),
+            dma((3 * NY + 1,)), dma((3 * NY + 1,)),
+            dma((NX - 1, NZ)), dma((NX, NZ)), dma((N_BLK,)), dma((N_BLK,)),
+            dma((N_BLK, NY - 1)), dma((N_BLK, NY)), dma((N_BLK, NX - 1)), dma((N_BLK, NX)),
             dma((NX - 1,)), dma((NX,)), dma((3, NZ)), dma((3, NZ)),
         ],
         compiler_params=pltpu.CompilerParams(
-            collective_id=0, has_side_effects=True, vmem_limit_bytes=50 * 1024 * 1024
+            collective_id=0, has_side_effects=True, vmem_limit_bytes=60 * 1024 * 1024
         ),
         name="attention_grads",
     )(queries, keys, values, outputs, grad_out, log_sums, doc_ids)
+    return copied(grads)
 
 
 def solution(mesh):

time: 91.4 us -> 82.5 us (0.903)
  the two profiles are of different devices: /device:TPU:33 before, /device:TPU:1 now
where the time goes in v3:
time: 82.5 us; the launch traced here: 81.8 us
  Pallas kernels  81.2 us (98%)
    pallas_call x1, Pallas kernels, per_device(): pl.pallas_call(kernel, out_shape=(out, out, out), in_specs=[pl.BlockSpec(...  79.5 us
    pallas_call x1, Pallas kernels, copied(): pl.pallas_call(copy_kernel, out_shape=(out,) * 3, in_specs=[vmem] * 3, ou...  1.7 us

profile of v3, /device:TPU:1, one launch (start us, length us, event | category | flops | bytes accessed | tf_op | source)
XLA Modules:
  0.0 81.8 jit_solution(971097998968076179)
XLA Ops:
  0.6 79.5 %attention_grads.1 = (bf16[24,2048]{1,0:T(8,128)(2,1)}, bf16[24,2048]{1,0:T(8,128)(2,1)}, bf16[24,2048]{1,0:T(8,128)(2,1)}) custom-call(bf16[24,2048]{1,0:T(8,128)(2,1)} %q.1, bf16[24,2048]{1,0:T(8,128)(2,1)} %k.1, bf16[24,2048]{1,0:T(8,128)(2,1)} %v.1, bf16[24,2048]{1,0:T(8,128)(2,1)} %o.1, bf16[24,2048]{1,0:T(8,128)(2,1)} %g.1, f32[1,384]{1,0:T(1,128)} %lse.1, ...), custom_call_target="tpu_custom_call" | custom-call | tf_op jit(solution)/shard_map/attention_grads/pallas_call | solution.py:542
  80.1 1.7 %copy_grads.1 = (bf16[24,2048]{1,0:T(8,128)(2,1)}, bf16[24,2048]{1,0:T(8,128)(2,1)}, bf16[24,2048]{1,0:T(8,128)(2,1)}) custom-call(bf16[24,2048]{1,0:T(8,128)(2,1)} %get-tuple-element.6.a, bf16[24,2048]{1,0:T(8,128)(2,1)} %get-tuple-element.7.b, bf16[24,2048]{1,0:T(8,128)(2,1)} %get-tuple-element.8.c), custom_call_target="tpu_custom_call" | custom-call | tf_op jit(solution)/shard_map/copy_grads/pallas_call | solution.py:532

commit v4 on v3

--- a/solution.py
+++ b/solution.py
@@ -17,7 +17,6 @@
 Q_BLK = BLK * Q_Z
 K_BLK = BLK * K_Z
 PART = NY * ROWS
-STATS = CTX_ROWS + DH
 MESH = pl.DeviceIdType.MESH
 F32 = jnp.float32
 BF16 = jnp.bfloat16
@@ -66,7 +65,7 @@
 def kernel(
     q, k, v, o, g, lse, doc,
     oq, ok, ov,
-    Q, K, V, G, L, D, delta, stats, doc_in, lse_in, g_in, o_in,
+    Q, K, V, G, LH, L, D, delta, stats, doc_in, lse_in, g_in, o_in,
     qs, ks, vs, gs, kt, probs, lse_s, delta_s,
     dq, dk, dv, pq, rs, rq, rk, rv, res,
     z_send, z_recv, own, d_send, d_recv,
@@ -114,9 +113,9 @@
     )
 
     def lse_copy(frm):
-        return remote(stats, L.at[c, frm], hub_send, hub_recv.at[frm], device(x, y, plane, c))
-
-    lse_own = pltpu.make_async_copy(stats, L.at[c, z], own.at[4])
+        return remote(stats, LH.at[frm], hub_send, hub_recv.at[frm], device(x, y, plane, c))
+
+    lse_own = pltpu.make_async_copy(stats, LH.at[z], own.at[4])
 
     srcs = (q, k, g, v)
 
@@ -149,7 +148,6 @@
         loop(NZ - 1, lambda i: z_wait_from(a, i))
 
     z_start(0)
-    z_start(1)
 
     lane = lax.broadcasted_iota(jnp.int32, (ROWS, DH), 1)
     fetch[0].wait()
@@ -159,7 +157,8 @@
     for d in range(3):
         before = jnp.sum((numbers <= d).astype(F32), axis=1, keepdims=True)
         counts = jnp.where(lane[:1] == d, before, counts)
-    stats[...] = jnp.concatenate([lse_in[...], counts], axis=1)
+    for xx in range(NX):
+        stats[xx] = jnp.concatenate([lse_in[:, block(xx, PART)], counts[:, : DH - PART]], axis=1)
 
     @pl.when(hub)
     def _():
@@ -169,8 +168,7 @@
     def _():
         lse_copy(z).start()
 
-    z_start(2)
-    z_start(3)
+    z_start(1)
 
     fetch[2].wait()
     fetch[3].wait()
@@ -191,6 +189,8 @@
     delta_own = pltpu.make_async_copy(delta.at[z], D.at[z, c, y], own.at[6])
     delta_own.start()
     loop(NZ - 1, lambda i: delta_copy(i, ring(z, i, NZ), z).start())
+    z_start(2)
+    z_start(3)
 
     def sib_copy(part, slot):
         return remote(part, part, s_send.at[slot], s_recv.at[slot], sib)
@@ -239,11 +239,17 @@
         loop(last - first, one)
 
     def plane_copy(i):
-        return remote(L.at[c], L.at[c], plane_send.at[i], plane_recv, plane_peer(i))
+        other = lax.rem(plane + i + 1, NX * NY)
+        return remote(
+            LH.at[:, lax.div(other, NY)], L.at[c], plane_send.at[i], plane_recv, plane_peer(i)
+        )
 
     def lse_sib(core):
         return sib_copy(L.at[core], 3 * NY)
 
+    z_wait(0)
+    y_start(0)
+
     @pl.when(hub)
     def _():
         lse_own.wait()
@@ -253,27 +259,30 @@
 
         loop(NZ - 1, one)
         loop(NX * NY - 1, lambda i: plane_copy(i).start())
-
-    z_wait(0)
-    y_start(0)
+        pltpu.make_async_copy(LH.at[:, x], L.at[c], own.at[5]).start()
+
     z_wait(1)
     for i in range(NX - 1):
         x_copy(i, x, ring(x, i, NX)).start()
 
+    @pl.when(hub)
+    def _():
+        pltpu.make_async_copy(LH.at[:, x], L.at[c], own.at[5]).wait()
+
     @pl.when(jnp.logical_not(hub))
     def _():
         plane_copy(0).wait_recv()
 
     lse_sib(c).start()
-    z_wait(2)
-    y_start(1)
-    y_relay(0)
     delta_own.wait()
     loop(NZ - 1, lambda i: delta_copy(i, z, ring(z, i, NZ)).wait_recv())
     y_start(2)
+    y_relay(0)
+    z_wait(2)
+    y_start(1)
     lse_sib(1 - c).wait_recv()
     rows = [jnp.concatenate([L[core, zz] for zz in range(NZ)], axis=0) for core in range(NC)]
-    counts = rows[0][:, CTX_ROWS:] + rows[1][:, CTX_ROWS:]
+    counts = rows[0][:, PART:] + rows[1][:, PART:]
     ends = [jnp.sum(counts[:, d : d + 1]).astype(jnp.int32) for d in range(3)]
 
     def doc_start(pos):
@@ -285,13 +294,7 @@
         for j in range(N_BLK):
             out[j] = jnp.concatenate([by_plane[zz : zz + 1] for zz in range(BLK * j, BLK * (j + 1))], axis=1)
 
-    parts = []
-    for core in range(NC):
-        picked = rows[core][:, :PART]
-        for xx in range(1, NX):
-            picked = jnp.where(x == xx, rows[core][:, block(xx, PART)], picked)
-        parts.append(picked)
-    lay_rows(jnp.concatenate(parts, axis=1), lse_s)
+    lay_rows(jnp.concatenate([of_core[:, :PART] for of_core in rows], axis=1), lse_s)
 
     q_at = lax.broadcasted_iota(jnp.int32, (1, Q_BLK), 1)
     q_in = lax.rem(q_at, Q_Z)
@@ -546,9 +549,9 @@
         out_specs=(hbm,) * 3,
         scratch_shapes=[
             pltpu.VMEM(qg, BF16), pltpu.VMEM(kv, BF16), pltpu.VMEM(kv, BF16), pltpu.VMEM(qg, BF16),
-            pltpu.VMEM((NC, NZ, 1, STATS), F32),
+            pltpu.VMEM((NZ, NX, 1, DH), F32), pltpu.VMEM((NC, NZ, 1, DH), F32),
             pltpu.VMEM((NZ, NC, NY, 1, DH), F32),
-            pltpu.VMEM((NZ, 1, DH), F32), pltpu.VMEM((1, STATS), F32),
+            pltpu.VMEM((NZ, 1, DH), F32), pltpu.VMEM((NX, 1, DH), F32),
             pltpu.VMEM((CTX_ROWS,), jnp.int32), pltpu.VMEM((1, CTX_ROWS), F32), pltpu.VMEM((ROWS, NZ * DH), BF16), pltpu.VMEM((ROWS, NZ * DH), BF16),
             pltpu.VMEM((NZ * Q_Z, DH), BF16), pltpu.VMEM((NZ * K_Z, DH), BF16),
             pltpu.VMEM((NZ * K_Z, DH), BF16), pltpu.VMEM((NZ * Q_Z, DH), BF16),

time: 82.5 us -> 79.4 us (0.962)
  Pallas kernels: 81.2 us -> 77.7 us
    pallas_call x1, Pallas kernels: 79.5 us -> 76 us  [per_device(): pl.pallas_call(kernel, out_shape=(out, out, out), in_specs=[pl.BlockSpec(...]
where the time goes in v4:
time: 79.4 us; the launch traced here: 78.3 us
  Pallas kernels  77.7 us (98%)
    pallas_call x1, Pallas kernels, per_device(): pl.pallas_call(kernel, out_shape=(out, out, out), in_specs=[pl.BlockSpec(...  76 us
    pallas_call x1, Pallas kernels, copied(): pl.pallas_call(copy_kernel, out_shape=(out,) * 3, in_specs=[vmem] * 3, ou...  1.7 us

profile of v4, /device:TPU:1, one launch (start us, length us, event | category | flops | bytes accessed | tf_op | source)
XLA Modules:
  0.0 78.3 jit_solution(18259720709873433281)
XLA Ops:
  0.6 76.0 %attention_grads.1 = (bf16[24,2048]{1,0:T(8,128)(2,1)}, bf16[24,2048]{1,0:T(8,128)(2,1)}, bf16[24,2048]{1,0:T(8,128)(2,1)}) custom-call(bf16[24,2048]{1,0:T(8,128)(2,1)} %q.1, bf16[24,2048]{1,0:T(8,128)(2,1)} %k.1, bf16[24,2048]{1,0:T(8,128)(2,1)} %v.1, bf16[24,2048]{1,0:T(8,128)(2,1)} %o.1, bf16[24,2048]{1,0:T(8,128)(2,1)} %g.1, f32[1,384]{1,0:T(1,128)} %lse.1, ...), custom_call_target="tpu_custom_call" | custom-call | tf_op jit(solution)/shard_map/attention_grads/pallas_call | solution.py:545
  76.6 1.7 %copy_grads.1 = (bf16[24,2048]{1,0:T(8,128)(2,1)}, bf16[24,2048]{1,0:T(8,128)(2,1)}, bf16[24,2048]{1,0:T(8,128)(2,1)}) custom-call(bf16[24,2048]{1,0:T(8,128)(2,1)} %get-tuple-element.6.a, bf16[24,2048]{1,0:T(8,128)(2,1)} %get-tuple-element.7.b, bf16[24,2048]{1,0:T(8,128)(2,1)} %get-tuple-element.8.c), custom_call_target="tpu_custom_call" | custom-call | tf_op jit(solution)/shard_map/copy_grads/pallas_call | solution.py:535

commit v5 on v4

--- a/solution.py
+++ b/solution.py
@@ -32,8 +32,25 @@
 
 
 def ring(me, step, size):
-    away = lax.div(step, 2) + 1
-    return lax.rem(jnp.where(lax.rem(step, 2) == 0, me + away, me - away + size), size)
+    away, up = step if isinstance(step, tuple) else (step // 2 + 1, step % 2 == 0)
+    if up:
+        return jnp.where(me + away >= size, me + away - size, me + away)
+    return jnp.where(me < away, me - away + size, me - away)
+
+
+def slot(step):
+    away, up = step
+    return 2 * (away - 1) + (0 if up else 1)
+
+
+def peers(body):
+    def step(i, carry):
+        body((i + 1, True))
+        body((i + 1, False))
+        return carry
+
+    lax.fori_loop(0, NZ // 2 - 1, step, 0)
+    body((NZ // 2, True))
 
 
 def columns(head):
@@ -64,7 +81,7 @@
 
 def kernel(
     q, k, v, o, g, lse, doc,
-    oq, ok, ov,
+    grads,
     Q, K, V, G, LH, L, D, delta, stats, doc_in, lse_in, g_in, o_in,
     qs, ks, vs, gs, kt, probs, lse_s, delta_s,
     dq, dk, dv, pq, rs, rq, rk, rv, res,
@@ -89,15 +106,16 @@
         other = lax.rem(plane + i + 1, NX * NY)
         return device(lax.div(other, NY), lax.rem(other, NY), z, c)
 
-    loop(NZ - 1, lambda i: greet(device(x, y, ring(z, i, NZ), c)))
+    peers(lambda i: greet(device(x, y, ring(z, i, NZ), c)))
     fetch = [
         pltpu.make_async_copy(src, dst, own.at[10 + i])
         for i, (src, dst) in enumerate(((doc, doc_in), (lse, lse_in), (g, g_in), (o, o_in)))
     ]
     for copy in fetch:
         copy.start()
-    loop(NX - 1, lambda i: greet(device(ring(x, i, NX), y, z, c)))
-    loop(NY - 1, lambda i: greet(device(x, ring(y, i, NY), z, c)))
+    for i in range(NX - 1):
+        greet(device(ring(x, i, NX), y, z, c))
+        greet(device(x, ring(y, i, NY), z, c))
     greet(sib)
 
     @pl.when(hub)
@@ -125,7 +143,7 @@
     def z_copy(a, i):
         to = ring(z, i, NZ)
         return remote(
-            srcs[a].at[:, columns(to)], landing(a, z), z_send.at[a, i], z_recv.at[a, z],
+            srcs[a].at[:, columns(to)], landing(a, z), z_send.at[a, slot(i)], z_recv.at[a, z],
             device(x, y, to, c),
         )
 
@@ -134,18 +152,18 @@
 
     def z_start(a):
         own_copy(a).start()
-        loop(NZ - 1, lambda i: z_copy(a, i).start())
+        peers(lambda i: z_copy(a, i).start())
 
     def z_wait_from(a, i):
         frm = ring(z, i, NZ)
         remote(
-            srcs[a].at[:, columns(frm)], landing(a, frm), z_send.at[a, i], z_recv.at[a, frm],
+            srcs[a].at[:, columns(frm)], landing(a, frm), z_send.at[a, slot(i)], z_recv.at[a, frm],
             device(x, y, frm, c),
         ).wait_recv()
 
     def z_wait(a):
         own_copy(a).wait()
-        loop(NZ - 1, lambda i: z_wait_from(a, i))
+        peers(lambda i: z_wait_from(a, i))
 
     z_start(0)
 
@@ -183,12 +201,12 @@
 
     def delta_copy(i, to, frm):
         return remote(
-            delta.at[to], D.at[frm, c, y], d_send.at[i], d_recv.at[frm], device(x, y, ring(z, i, NZ), c)
+            delta.at[to], D.at[frm, c, y], d_send.at[slot(i)], d_recv.at[frm], device(x, y, ring(z, i, NZ), c)
         )
 
     delta_own = pltpu.make_async_copy(delta.at[z], D.at[z, c, y], own.at[6])
     delta_own.start()
-    loop(NZ - 1, lambda i: delta_copy(i, ring(z, i, NZ), z).start())
+    peers(lambda i: delta_copy(i, ring(z, i, NZ), z).start())
     z_start(2)
     z_start(3)
 
@@ -231,12 +249,12 @@
         for i in range(NX - 1):
             xv_copy(i, zs, x, ring(x, i, NX)).start()
 
-    def pass_values(first, last):
+    def pass_values():
         def one(i):
-            z_wait_from(3, first + i)
-            xv_start(ring(z, first + i, NZ))
-
-        loop(last - first, one)
+            z_wait_from(3, i)
+            xv_start(ring(z, i, NZ))
+
+        peers(one)
 
     def plane_copy(i):
         other = lax.rem(plane + i + 1, NX * NY)
@@ -257,7 +275,7 @@
         def one(i):
             lse_copy(ring(z, i, NZ)).wait_recv()
 
-        loop(NZ - 1, one)
+        peers(one)
         loop(NX * NY - 1, lambda i: plane_copy(i).start())
         pltpu.make_async_copy(LH.at[:, x], L.at[c], own.at[5]).start()
 
@@ -275,7 +293,7 @@
 
     lse_sib(c).start()
     delta_own.wait()
-    loop(NZ - 1, lambda i: delta_copy(i, z, ring(z, i, NZ)).wait_recv())
+    peers(lambda i: delta_copy(i, z, ring(z, i, NZ)).wait_recv())
     y_start(2)
     y_relay(0)
     z_wait(2)
@@ -340,9 +358,8 @@
     probs_block(1)
     own_copy(3).wait()
     xv_start(z)
-    pass_values(0, 8)
+    pass_values()
     probs_block(2)
-    pass_values(8, NZ - 1)
     y_relay(1)
     probs_block(3)
     y_relay(2)
@@ -406,16 +423,18 @@
         for i in range(NX - 1):
             k_copy(j, i, x, ring(x, i, NX)).start()
 
-    outs = (oq, ok, ov)
+    parts_of = (pl.ds(0, 2), pl.ds(2, 1))
 
     def home_copy(a, to, frm):
         return remote(
-            res.at[a, to], outs[a].at[:, columns(frm)], h_send.at[a, to], h_recv.at[a, frm],
-            device(x, y, to, c),
+            res.at[parts_of[a], to], grads.at[parts_of[a], :, columns(frm)],
+            h_send.at[a, to], h_recv.at[a, frm], device(x, y, to, c),
         )
 
     def home_own(a):
-        return pltpu.make_async_copy(res.at[a, z], outs[a].at[:, columns(z)], own.at[7 + a])
+        return pltpu.make_async_copy(
+            res.at[parts_of[a], z], grads.at[parts_of[a], :, columns(z)], own.at[7 + a]
+        )
 
     def send_home(a, to):
         @pl.when(to == z)
@@ -437,7 +456,8 @@
             res[2, zz] = total.astype(BF16)
 
         loop(NZ, one)
-        loop(NZ, lambda i: send_home(2, lax.rem(z + i, NZ)))
+        home_own(1).start()
+        peers(lambda i: home_copy(1, ring(z, i, NZ), z).start())
 
     def pair_block(j):
         p_copy(j, c).wait_recv()
@@ -466,7 +486,6 @@
             for i in range(NY - 1):
                 total += rq[ring(y, i, NY), zz].astype(F32)
             res[0, zz] = (total * scale).astype(BF16)
-            send_home(1, zz)
             send_home(0, zz)
 
         loop(BLK, one)
@@ -486,8 +505,8 @@
     add_block(0)
 
     for a in range(4):
-        loop(NZ - 1, lambda i, a=a: z_copy(a, i).wait_send())
-    loop(NZ - 1, lambda i: delta_copy(i, ring(z, i, NZ), z).wait_send())
+        peers(lambda i, a=a: z_copy(a, i).wait_send())
+    peers(lambda i: delta_copy(i, ring(z, i, NZ), z).wait_send())
 
     @pl.when(jnp.logical_not(hub))
     def _():
@@ -514,7 +533,7 @@
         for i in range(NY - 1):
             q_copy(j, i, y, ring(y, i, NY)).wait_send()
         p_copy(j, 1 - c).wait_send()
-    for a in range(3):
+    for a in (1, 0):
         home_own(a).wait()
 
         def one(i, a=a):
@@ -522,31 +541,31 @@
             home_copy(a, peer, z).wait_send()
             home_copy(a, z, peer).wait_recv()
 
-        loop(NZ - 1, one)
-
-
-def copy_kernel(a, b, c, out_a, out_b, out_c):
-    out_a[...], out_b[...], out_c[...] = a[...], b[...], c[...]
+        peers(one)
+
+
+def copy_kernel(grads, out_q, out_k, out_v):
+    for i, out in enumerate((out_q, out_k, out_v)):
+        out[...] = grads[i]
 
 
 def copied(grads):
     vmem = pl.BlockSpec(memory_space=pltpu.VMEM)
     out = jax.ShapeDtypeStruct((ROWS, NZ * DH), BF16)
     return pl.pallas_call(
-        copy_kernel, out_shape=(out,) * 3, in_specs=[vmem] * 3, out_specs=(vmem,) * 3, name="copy_grads"
-    )(*grads)
+        copy_kernel, out_shape=(out,) * 3, in_specs=[vmem], out_specs=(vmem,) * 3, name="copy_grads"
+    )(grads)
 
 
 def per_device(queries, keys, values, outputs, grad_out, log_sums, doc_ids):
     dma = pltpu.SemaphoreType.DMA
     hbm = pl.BlockSpec(memory_space=pl.ANY)
-    out = jax.ShapeDtypeStruct((ROWS, NZ * DH), BF16)
     kv, qg = (NZ, NX, ROWS, DH), (NZ, NC, NY, ROWS, DH)
     grads = pl.pallas_call(
         kernel,
-        out_shape=(out, out, out),
+        out_shape=jax.ShapeDtypeStruct((3, ROWS, NZ * DH), BF16),
         in_specs=[pl.BlockSpec(memory_space=pltpu.HBM)] * 7,
-        out_specs=(hbm,) * 3,
+        out_specs=hbm,
         scratch_shapes=[
             pltpu.VMEM(qg, BF16), pltpu.VMEM(kv, BF16), pltpu.VMEM(kv, BF16), pltpu.VMEM(qg, BF16),
             pltpu.VMEM((NZ, NX, 1, DH), F32), pltpu.VMEM((NC, NZ, 1, DH), F32),
@@ -569,7 +588,7 @@
             dma((3 * NY + 1,)), dma((3 * NY + 1,)),
             dma((NX - 1, NZ)), dma((NX, NZ)), dma((N_BLK,)), dma((N_BLK,)),
             dma((N_BLK, NY - 1)), dma((N_BLK, NY)), dma((N_BLK, NX - 1)), dma((N_BLK, NX)),
-            dma((NX - 1,)), dma((NX,)), dma((3, NZ)), dma((3, NZ)),
+            dma((NX - 1,)), dma((NX,)), dma((2, NZ)), dma((2, NZ)),
         ],
         compiler_params=pltpu.CompilerParams(
             collective_id=0, has_side_effects=True, vmem_limit_bytes=60 * 1024 * 1024

time: 79.4 us -> 78.4 us (0.987)
  no operation moved by 1% of the time
where the time goes in v5:
time: 78.4 us; the launch traced here: 77.8 us
  Pallas kernels  77.2 us (98%)
    pallas_call x1, Pallas kernels, per_device(): pl.pallas_call(kernel, out_shape=jax.ShapeDtypeStruct((3, ROWS, NZ * DH),...  75.5 us
    pallas_call x1, Pallas kernels, copied(): pl.pallas_call(copy_kernel, out_shape=(out,) * 3, in_specs=[vmem], out_sp...  1.67 us

profile of v5, /device:TPU:1, one launch (start us, length us, event | category | flops | bytes accessed | tf_op | source)
XLA Modules:
  0.0 77.8 jit_solution(2603054608996894007)
XLA Ops:
  0.6 75.5 %attention_grads.1.grads = bf16[3,24,2048]{2,1,0:T(8,128)(2,1)} custom-call(bf16[24,2048]{1,0:T(8,128)(2,1)} %q.1, bf16[24,2048]{1,0:T(8,128)(2,1)} %k.1, bf16[24,2048]{1,0:T(8,128)(2,1)} %v.1, bf16[24,2048]{1,0:T(8,128)(2,1)} %o.1, bf16[24,2048]{1,0:T(8,128)(2,1)} %g.1, f32[1,384]{1,0:T(1,128)} %lse.1, s32[384]{0:T(512)} %doc.1), custom_call_target="tpu_custom_call" | custom-call | tf_op jit(solution)/shard_map/attention_grads/pallas_call | solution.py:564
  76.1 1.7 %copy_grads.1 = (bf16[24,2048]{1,0:T(8,128)(2,1)}, bf16[24,2048]{1,0:T(8,128)(2,1)}, bf16[24,2048]{1,0:T(8,128)(2,1)}) custom-call(bf16[3,24,2048]{2,1,0:T(8,128)(2,1)} %attention_grads.1.grads), custom_call_target="tpu_custom_call" | custom-call | tf_op jit(solution)/shard_map/copy_grads/pallas_call | solution.py:555

commit v6 on v5

--- a/solution.py
+++ b/solution.py
@@ -45,12 +45,12 @@
 
 def peers(body):
     def step(i, carry):
-        body((i + 1, True))
-        body((i + 1, False))
+        body((NZ // 2 - 1 - i, True))
+        body((NZ // 2 - 1 - i, False))
         return carry
 
+    body((NZ // 2, True))
     lax.fori_loop(0, NZ // 2 - 1, step, 0)
-    body((NZ // 2, True))
 
 
 def columns(head):

time: 78.4 us -> 75.5 us (0.963)
  Pallas kernels: 77.2 us -> 74 us
    pallas_call x1, Pallas kernels: 75.5 us -> 72.3 us  [per_device(): pl.pallas_call(kernel, out_shape=jax.ShapeDtypeStruct((3, ROWS, NZ * DH),...]
where the time goes in v6:
time: 75.5 us; the launch traced here: 74.7 us
  Pallas kernels  74 us (98%)
    pallas_call x1, Pallas kernels, per_device(): pl.pallas_call(kernel, out_shape=jax.ShapeDtypeStruct((3, ROWS, NZ * DH),...  72.3 us
    pallas_call x1, Pallas kernels, copied(): pl.pallas_call(copy_kernel, out_shape=(out,) * 3, in_specs=[vmem], out_sp...  1.67 us

profile of v6, /device:TPU:1, one launch (start us, length us, event | category | flops | bytes accessed | tf_op | source)
XLA Modules:
  0.0 74.7 jit_solution(17845455406300882464)
XLA Ops:
  0.6 72.3 %attention_grads.1.grads = bf16[3,24,2048]{2,1,0:T(8,128)(2,1)} custom-call(bf16[24,2048]{1,0:T(8,128)(2,1)} %q.1, bf16[24,2048]{1,0:T(8,128)(2,1)} %k.1, bf16[24,2048]{1,0:T(8,128)(2,1)} %v.1, bf16[24,2048]{1,0:T(8,128)(2,1)} %o.1, bf16[24,2048]{1,0:T(8,128)(2,1)} %g.1, f32[1,384]{1,0:T(1,128)} %lse.1, s32[384]{0:T(512)} %doc.1), custom_call_target="tpu_custom_call" | custom-call | tf_op jit(solution)/shard_map/attention_grads/pallas_call | solution.py:564
  73.0 1.7 %copy_grads.1 = (bf16[24,2048]{1,0:T(8,128)(2,1)}, bf16[24,2048]{1,0:T(8,128)(2,1)}, bf16[24,2048]{1,0:T(8,128)(2,1)}) custom-call(bf16[3,24,2048]{2,1,0:T(8,128)(2,1)} %attention_grads.1.grads), custom_call_target="tpu_custom_call" | custom-call | tf_op jit(solution)/shard_map/copy_grads/pallas_call | solution.py:555
